TPU v7x, 128 devices: a whole 4x4x4 slice. The times are simulated.
128 devices in a mesh: dp: 4 (over y), tensor: 32 (over z, x, core).
Axes of the slice: x: 4, y: 4, z: 4, core: 2. Of those that a mesh axis runs over, the one named last changes fastest.
Arguments:
- prompt_states: bfloat16 [8, 512, 2048], P('dp', 'tensor')
- decode_states: bfloat16 [128, 2048], P(('dp', 'tensor'))
- cache: bfloat16 [2, 136, 1536, 2048], P(None, 'dp', 'tensor'), may hold values from -160 to 160
- prompt_starts: int32 [8], replicated, may hold values from 0 to 1536, as said below
- decode_lengths: int32 [128], replicated, may hold values from 1 to 1536, as said below
- decode_slots: int32 [128], replicated, may hold values from 0 to 127, each once
- w_qkv: bfloat16 [3, 2048, 2048], P(None, None, 'tensor')
- w_out: bfloat16 [2048, 2048], P('tensor')
- w_gate_up: bfloat16 [2, 2048, 8192], P(None, None, 'tensor')
- w_down: bfloat16 [8192, 2048], P('tensor')
- gains: float32 [4, 2048], replicated, may hold values from 0.25 to 1.75
Outputs:
- prompt_out: bfloat16 [8, 512, 2048], P('dp', 'tensor')
- decode_out: bfloat16 [128, 2048], P(('dp', 'tensor'))
- new_prompt_kv: bfloat16 [2, 8, 512, 2048], P(None, 'dp', 'tensor')
- new_decode_kv: bfloat16 [2, 128, 2048], P(None, ('dp', 'tensor'))
Inputs may be any that keep to these rules, and one draw needn't show every extreme that they name: Decode request e sits in decode slot decode_slots[e]; each slot holds one request. `prompt_starts`: some prompt has exactly 1536 cached positions. `decode_lengths`: some decode request has exactly 1536 cached positions.
All inputs are finite; a program needn't handle non-finite values.
Results may differ from a plain program's by a relative error of at most 0.02.
Values may be sent and summed in bfloat16 or wider, within the bound.
A program may use at most 256 MiB of HBM per device.

v0:
```python
import jax
import jax.numpy as jnp
from jax import lax
from jax.sharding import PartitionSpec as P

HD = 128


EPSILON = 1e-06
ROPE_BASE = 500000.0
MASKED_SCORE = -1e30


def rms_scale(values, gain_vec):
    return (
        values * lax.rsqrt(jnp.mean(values * values, axis=-1, keepdims=True) + EPSILON) * gain_vec
    )


def rotate(values, positions):
    full_shape = values.shape
    paired = values.reshape(full_shape[:-1] + (full_shape[-1] // HD, HD // 2, 2))
    freq_index = jnp.arange(HD // 2, dtype=jnp.float32)
    inv_freq = jnp.power(ROPE_BASE, -2.0 * freq_index / HD)
    angles = positions.astype(jnp.float32)[..., None, None] * inv_freq
    cosine = jnp.cos(angles)
    sine_values = jnp.sin(angles)
    even_part = paired[..., 0]
    odd_part = paired[..., 1]
    turned = jnp.stack(
        [even_part * cosine - odd_part * sine_values, even_part * sine_values + odd_part * cosine],
        axis=-1,
    )
    return turned.reshape(full_shape)


def split_rows(stacked, tensors, pre_dev, part_rows):
    tail_shape = stacked.shape[1:]
    per_device = stacked.shape[0] // tensors
    device_grid = stacked.reshape((tensors, per_device) + tail_shape)
    prompt_part = device_grid[:, : pre_dev * part_rows].reshape(
        (tensors, pre_dev, part_rows) + tail_shape
    )
    prompt_part = jnp.swapaxes(prompt_part, 0, 1).reshape(
        (pre_dev, tensors * part_rows) + tail_shape
    )
    decode_part = device_grid[:, pre_dev * part_rows :].reshape((-1,) + tail_shape)
    return (prompt_part, decode_part)


def join_rows(prompt_part, decode_part, tensors):
    pre_dev = prompt_part.shape[0]
    part_rows = prompt_part.shape[1] // tensors
    tail_shape = prompt_part.shape[2:]
    leading = jnp.swapaxes(prompt_part.reshape((pre_dev, tensors, part_rows) + tail_shape), 0, 1)
    leading = leading.reshape((tensors, pre_dev * part_rows) + tail_shape)
    trailing = decode_part.reshape((tensors, -1) + tail_shape)
    return jnp.concatenate([leading, trailing], axis=1).reshape((-1,) + tail_shape)


def spread(local_rows, weights):
    return jnp.einsum(
        "rd,kdc->rkc",
        lax.all_gather(local_rows, "tensor", axis=0, tiled=True),
        weights,
        preferred_element_type=jnp.float32,
    )


def collect(operand, weights):
    return lax.psum_scatter(
        jnp.dot(operand, weights, preferred_element_type=jnp.float32).astype(jnp.bfloat16),
        "tensor",
        scatter_dimension=0,
        tiled=True,
    ).astype(jnp.float32)


def local(
    prompt_states,
    decode_states,
    cache,
    prompt_starts,
    decode_lengths,
    decode_slots,
    w_qkv,
    w_out,
    w_gate_up,
    w_down,
    gains,
):
    tensors = lax.axis_size("tensor")
    tensor_pos = lax.axis_index("tensor")
    data_pos = lax.axis_index("dp")
    pre_dev, part_rows, model_width = prompt_states.shape
    dec_part = decode_states.shape[0]
    group_len = part_rows * tensors
    dec_dev = dec_part * tensors
    ctx_part = cache.shape[2]
    head_count = model_width // HD
    prompt_own = pre_dev * part_rows
    own_rows = prompt_own + dec_part
    states = jnp.concatenate(
        [prompt_states.reshape(prompt_own, model_width), decode_states], axis=0
    )
    starts = lax.dynamic_slice_in_dim(prompt_starts, data_pos * pre_dev, pre_dev)
    slot_ids = data_pos * dec_dev + jnp.arange(dec_dev, dtype=jnp.int32)
    matches = decode_slots[None, :] == slot_ids[:, None]
    slot_length = jnp.sum(jnp.where(matches, decode_lengths[None, :], 0), axis=1)
    offsets = jnp.arange(group_len, dtype=jnp.int32)
    prompt_pos = starts[:, None] + offsets[None, :]
    own_prompt_pos = lax.dynamic_slice_in_dim(
        prompt_pos, tensor_pos * part_rows, part_rows, 1
    ).reshape(prompt_own)
    own_decode_pos = lax.dynamic_slice_in_dim(slot_length, tensor_pos * dec_part, dec_part)
    own_pos = jnp.concatenate([own_prompt_pos, own_decode_pos], axis=0)
    projected = spread(states, w_qkv)
    query_raw = projected[:, 0].astype(jnp.bfloat16)
    key_raw = projected[:, 1].astype(jnp.bfloat16)
    value_raw = projected[:, 2].astype(jnp.bfloat16)
    query_all, key_all, value_all = (
        lax.all_gather(query_raw, "tensor", axis=1, tiled=True),
        lax.all_gather(key_raw, "tensor", axis=1, tiled=True),
        lax.all_gather(value_raw, "tensor", axis=1, tiled=True),
    )
    key_own = lax.dynamic_slice_in_dim(key_all, tensor_pos * own_rows, own_rows, 0)
    value_own = lax.dynamic_slice_in_dim(value_all, tensor_pos * own_rows, own_rows, 0)
    query_prompt, query_decode = split_rows(query_all, tensors, pre_dev, part_rows)
    query_prompt = rotate(rms_scale(query_prompt.astype(jnp.float32), gains[0]), prompt_pos).astype(
        jnp.bfloat16
    )
    query_decode = rotate(
        rms_scale(query_decode.astype(jnp.float32), gains[0]), slot_length
    ).astype(jnp.bfloat16)
    key_new = rotate(rms_scale(key_own.astype(jnp.float32), gains[1]), own_pos).astype(jnp.bfloat16)
    scale_factor = HD ** (-0.5)
    cache_pos = tensor_pos * ctx_part + jnp.arange(ctx_part, dtype=jnp.int32)
    prompt_q = query_prompt.reshape(pre_dev, group_len, head_count, HD)
    prompt_keys = cache[0, :pre_dev].reshape(pre_dev, ctx_part, head_count, HD)
    prompt_values = cache[1, :pre_dev].reshape(pre_dev, ctx_part, head_count, HD)
    fresh_keys = key_new[:prompt_own].reshape(pre_dev, part_rows, head_count, HD)
    fresh_values = value_own[:prompt_own].reshape(pre_dev, part_rows, head_count, HD)
    cached_scores = jnp.einsum(
        "aihe,ajhe->ahij", prompt_q, prompt_keys, preferred_element_type=jnp.float32
    )
    fresh_scores = jnp.einsum(
        "aihe,ajhe->ahij", prompt_q, fresh_keys, preferred_element_type=jnp.float32
    )
    prompt_scores = jnp.concatenate([cached_scores, fresh_scores], axis=-1) * scale_factor
    key_offsets = tensor_pos * part_rows + jnp.arange(part_rows, dtype=jnp.int32)
    live_cached = jnp.broadcast_to(
        (cache_pos[None, :] < starts[:, None])[:, None, None, :], (pre_dev, 1, group_len, ctx_part)
    )
    live_fresh = jnp.broadcast_to(
        (key_offsets[None, :] <= offsets[:, None])[None, None], (pre_dev, 1, group_len, part_rows)
    )
    prompt_live = jnp.concatenate([live_cached, live_fresh], axis=-1)
    prompt_masked = jnp.where(prompt_live, prompt_scores, MASKED_SCORE)
    prompt_top = jnp.max(prompt_masked, axis=-1)
    decode_q = query_decode.reshape(dec_dev, head_count, HD)
    decode_keys = cache[0, pre_dev:].reshape(dec_dev, ctx_part, head_count, HD)
    decode_values = cache[1, pre_dev:].reshape(dec_dev, ctx_part, head_count, HD)
    own_keys = key_new[prompt_own:].reshape(dec_part, head_count, HD)
    own_values = value_own[prompt_own:].reshape(dec_part, head_count, HD)
    decode_cached = jnp.einsum(
        "she,sjhe->shj", decode_q, decode_keys, preferred_element_type=jnp.float32
    )
    decode_fresh = jnp.einsum(
        "she,jhe->shj", decode_q, own_keys, preferred_element_type=jnp.float32
    )
    decode_scores = jnp.concatenate([decode_cached, decode_fresh], axis=-1) * scale_factor
    live_slots = (cache_pos[None, :] < slot_length[:, None])[:, None, :]
    own_ids = tensor_pos * dec_part + jnp.arange(dec_part, dtype=jnp.int32)
    live_owned = (jnp.arange(dec_dev, dtype=jnp.int32)[:, None] == own_ids[None, :])[:, None, :]
    decode_live = jnp.concatenate([live_slots, live_owned], axis=-1)
    decode_masked = jnp.where(decode_live, decode_scores, MASKED_SCORE)
    decode_top = jnp.max(decode_masked, axis=-1)
    prompt_weights = jnp.where(prompt_live, jnp.exp(prompt_masked - prompt_top[..., None]), 0.0)
    prompt_total = jnp.sum(prompt_weights, axis=-1)
    prompt_probs = prompt_weights.astype(jnp.bfloat16)
    prompt_mixed = jnp.einsum(
        "ahij,ajhe->aihe",
        prompt_probs[..., :ctx_part],
        prompt_values,
        preferred_element_type=jnp.float32,
    )
    prompt_mixed = prompt_mixed + jnp.einsum(
        "ahij,ajhe->aihe",
        prompt_probs[..., ctx_part:],
        fresh_values,
        preferred_element_type=jnp.float32,
    )
    decode_weights = jnp.where(decode_live, jnp.exp(decode_masked - decode_top[..., None]), 0.0)
    decode_total = jnp.sum(decode_weights, axis=-1)
    decode_probs = decode_weights.astype(jnp.bfloat16)
    decode_mixed = jnp.einsum(
        "shj,sjhe->she",
        decode_probs[..., :ctx_part],
        decode_values,
        preferred_element_type=jnp.float32,
    )
    decode_mixed = decode_mixed + jnp.einsum(
        "shj,jhe->she", decode_probs[..., ctx_part:], own_values, preferred_element_type=jnp.float32
    )
    totals = join_rows(jnp.swapaxes(prompt_total, 1, 2), decode_total, tensors)
    mixed = join_rows(
        prompt_mixed.reshape(pre_dev, group_len, model_width),
        decode_mixed.reshape(dec_dev, model_width),
        tensors,
    )
    tops = join_rows(jnp.swapaxes(prompt_top, 1, 2), decode_top, tensors)
    got_tops, got_totals, got_mixed = (
        lax.all_to_all(tops, "tensor", split_axis=0, concat_axis=0, tiled=True),
        lax.all_to_all(totals, "tensor", split_axis=0, concat_axis=0, tiled=True),
        lax.all_to_all(mixed, "tensor", split_axis=0, concat_axis=0, tiled=True),
    )
    got_tops = got_tops.reshape(tensors, own_rows, head_count)
    got_totals = got_totals.reshape(tensors, own_rows, head_count)
    got_mixed = got_mixed.reshape(tensors, own_rows, head_count, HD)
    highest = jnp.max(got_tops, axis=0)
    factors = jnp.exp(got_tops - highest[None])
    total_all = jnp.sum(got_totals * factors, axis=0)
    shares = lax.optimization_barrier((got_mixed * factors[..., None]).astype(jnp.bfloat16))
    mixed_all = jnp.sum(shares.astype(jnp.float32), axis=0)
    attended_own = (
        (mixed_all / total_all[..., None]).reshape(own_rows, model_width).astype(jnp.bfloat16)
    )
    my_columns = lax.all_to_all(attended_own, "tensor", split_axis=1, concat_axis=0, tiled=True)
    attn_sum = collect(my_columns, w_out)
    hidden = (states.astype(jnp.float32) + rms_scale(attn_sum, gains[2])).astype(jnp.bfloat16)
    gate_up = spread(hidden, w_gate_up)
    activated = (jax.nn.silu(gate_up[:, 0]) * gate_up[:, 1]).astype(jnp.bfloat16)
    ffn_sum = collect(activated, w_down)
    output = (hidden.astype(jnp.float32) + rms_scale(ffn_sum, gains[3])).astype(jnp.bfloat16)
    prompt_out = output[:prompt_own].reshape(pre_dev, part_rows, model_width)
    everyone = lax.all_gather(output[prompt_own:], ("dp", "tensor"), axis=0, tiled=True)
    wanted = lax.dynamic_slice_in_dim(
        decode_slots, (data_pos * tensors + tensor_pos) * dec_part, dec_part
    )
    decode_out = jnp.take(everyone, wanted, axis=0)
    new_prompt_kv = jnp.stack([key_new[:prompt_own], value_own[:prompt_own]]).reshape(
        2, pre_dev, part_rows, model_width
    )
    new_decode_kv = jnp.stack([key_new[prompt_own:], value_own[prompt_own:]])
    return (prompt_out, decode_out, new_prompt_kv, new_decode_kv)


def solution(mesh):
    in_specs = (
        P("dp", "tensor", None),
        P(("dp", "tensor"), None),
        P(None, "dp", "tensor", None),
        P(),
        P(),
        P(),
        P(None, None, "tensor"),
        P("tensor", None),
        P(None, None, "tensor"),
        P("tensor", None),
        P(),
    )
    out_specs = (
        P("dp", "tensor", None),
        P(("dp", "tensor"), None),
        P(None, "dp", "tensor", None),
        P(None, ("dp", "tensor"), None),
    )
    return jax.shard_map(local, mesh=mesh, in_specs=in_specs, out_specs=out_specs, check_vma=False)
```

profile of v0, /device:TPU:1, one launch (start us, length us, event | category | flops | bytes accessed | tf_op | source)
XLA Modules:
  0.0 949.0 jit_solution(1987351854359071454)
XLA Ops:
  7.2 1.7 fusion.37
  9.1 53.0 %all-gather.18.cloned.1.call-done = bf16[32,33,2048]{2,1,0:T(8,128)(2,1)} async-done(((bf16[1,33,2048]{2,1,0:T(8,128)(2,1)}), bf16[32,33,2048]{2,1,0:T(8,128)(2,1)}) %all-gather.18.cloned.1.call-update) | async-done | bytes 4325392 | tf_op jit(solution)/shard_map/all_gather | solution.py:64
  62.0 5.6 reshape.574
  67.7 4.0 fusion.46
  75.5 10.7 %fusion.43 = (bf16[1,32,48,2048]{3,2,1,0:T(8,128)(2,1)}, bf16[1,32,48,2048]{3,2,1,0:T(8,128)(2,1)}) fusion(bf16[2,34,48,2048]{3,2,1,0:T(8,128)(2,1)} %param.13), kind=kLoop, calls=%fused_computation.120 | loop fusion | bytes 25165824 | tf_op jit(solution)/shard_map/slice | solution.py:162
  89.1 8.1 copy.276
  97.2 5.0 copy.275
  104.2 1.8 multiply_cosine_fusion
  106.1 12.8 %all-gather.14.cloned.1.call-done = bf16[1056,1,2048]{0,2,1:T(8,128)(2,1)} async-done(((bf16[1056,1,64]{0,2,1:T(8,128)(2,1)}), bf16[1056,1,2048]{0,2,1:T(8,128)(2,1)}) %all-gather.14.cloned.1.call-update) | async-done | bytes 4325392 | tf_op jit(solution)/shard_map/all_gather | solution.py:123
  120.5 1.7 fusion.13
  122.2 1.9 fusion.44
  128.9 38.5 %all-gather.12.cloned.1.call-done = bf16[1056,1,2048]{0,2,1:T(8,128)(2,1)} async-done(((bf16[1056,1,64]{0,2,1:T(8,128)(2,1)}), bf16[1056,1,2048]{0,2,1:T(8,128)(2,1)}) %all-gather.12.cloned.1.call-update) | async-done | bytes 4325392 | tf_op jit(solution)/shard_map/all_gather | solution.py:122
  167.4 6.6 copy.207
  174.0 5.6 reshape.507
  182.6 3.2 multiply_multiply_fusion.1
  188.8 7.0 multiply_reduce_fusion
  199.7 3.1 multiply_reduce_fusion.1
  202.7 6.6 slice_convert_fusion
  209.3 7.0 all-gather.16.cloned.1.call-done
  216.4 2.2 constant_dynamic-slice_fusion
  219.9 1.7 copy.216
  221.6 3.2 reshape.509
  226.4 62.1 %copy.208 = f32[2,32,16,2048]{2,1,3,0:T(8,128)} copy(f32[2,32,16,2048]{3,2,0,1:T(8,128)} %bitcast.173) | data formatting | bytes 16777216 | tf_op jit(solution)/shard_map/convert_element_type | solution.py:129
  288.5 50.2 %reshape.542 = f32[2,512,16,64,2]{1,4,3,2,0:T(2,128)} reshape(f32[2,32,16,2048]{2,1,3,0:T(8,128)} %copy.208) | data formatting | bytes 16777216 | tf_op jit(solution)/shard_map/convert_element_type | solution.py:129
  338.7 5.8 multiply_multiply_fusion
  344.5 11.1 %subtract_convert_fusion = (bf16[2,512,16,64,1]{1,4,3,2,0:T(2,128)(2,1)S(1)}, bf16[2,512,16,64,1]{1,4,3,2,0:T(2,128)(2,1)S(1)}) fusion(f32[2,512,16,64,2]{1,4,3,2,0:T(2,128)S(1)} %multiply_multiply_fusion, f32[2,512,64]{1,2,0:T(8,128)S(1)} %copy-done.17, f32[2,512,64]{1,2,0:T(8,128)S(1)} %copy-done.16), kind=kLoop, calls=%fused_computation.19 | loop fusion | flops 8388608 | bytes 13107200 | tf_op jit(solution)/shard_map/convert.18
  355.6 8.9 pad_maximum_fusion.1
  364.5 6.5 copy.211
  371.0 8.0 copy.212
  379.1 3.6 fusion.14
  384.9 2.6 fusion.6
  389.1 5.8 all-to-all-start.1
  395.3 4.7 fusion.3
  401.3 4.7 bitcast_add_fusion
  406.0 2.1 convert_reduce_fusion.1
  409.4 11.5 %copy.223 = f32[2,512,16,128]{3,2,1,0:T(8,128)} copy(f32[2,512,16,128]{3,1,2,0:T(8,128)} %bitcast_add_fusion) | data formatting | bytes 16777216 | tf_op jit(solution)/shard_map/add | solution.py:187
  420.9 9.4 reshape_reshape.6
  430.2 7.8 copy.224
  438.0 7.4 all-to-all-start.2
  445.4 8.8 pad_maximum_fusion
  454.2 7.4 all-to-all-start
  465.0 122.6 %all-to-all-done = f32[32,33,2048]{2,1,0:T(8,128)} async-done(((f32[32,33,2048]{2,1,0:T(8,128)}), f32[32,33,2048]{2,1,0:T(8,128)}, u32[]{:S(2)}, u32[]{:S(2)}) %all-to-all-start) | async-done | bytes 8650784 | tf_op jit(solution)/shard_map/all_to_all | solution.py:215
  587.6 9.8 %reshape.592 = f32[32,33,16,128]{3,2,1,0:T(8,128)} reshape(f32[32,33,2048]{2,1,0:T(8,128)} %all-to-all-done) | data formatting | bytes 17301504 | tf_op jit(solution)/shard_map/reshape | solution.py:219
  597.4 5.3 fusion.2
  604.2 17.6 %all_to_all.34 = bf16[32,2,1056]{2,1,0:T(2,128)(2,1)S(1)} all-to-all(bf16[32,2,1056]{2,1,0:T(2,128)(2,1)S(1)} %reshape.608), channel_id=1, replica_groups=mesh['dp'=4,'tensor'=32] {'tensor'}, dimensions={0} | all-to-all | bytes 270336 | tf_op jit(solution)/shard_map/all_to_all | solution.py:228
  622.2 3.3 convolution_convert_fusion
  625.5 75.6 %fusion = bf16[40,2048]{1,0:T(8,128)(2,1)S(1)} fusion(bf16[1056,2048]{1,0:T(8,128)(2,1)} %convolution_convert_fusion), kind=kCustom, calls=%all-reduce-scatter | all-reduce-scatter fusion | flops 2621441 | bytes 4489728
  706.3 2.6 collective-permute-start.1
  709.0 2.4 collective-permute-start
  715.2 2.8 collective-permute-done
  718.1 6.4 concatenate.45
  724.6 1.8 fusion.41
  730.9 2.9 stack.39
  733.9 1.7 copy.246
  735.6 45.2 %all-gather.20.cloned.1.call-done = bf16[32,33,2048]{2,1,0:T(8,128)(2,1)} async-done(((bf16[1,33,2048]{2,1,0:T(8,128)(2,1)}), bf16[32,33,2048]{2,1,0:T(8,128)(2,1)}) %all-gather.20.cloned.1.call-update) | async-done | bytes 4325392 | tf_op jit(solution)/shard_map/all_gather | solution.py:64
  780.8 5.6 reshape.591
  786.3 4.7 fusion.48
  791.1 3.3 convolution_convert_fusion.1
  794.5 76.0 %fusion.1 = bf16[40,2048]{1,0:T(8,128)(2,1)S(1)} fusion(bf16[1056,2048]{1,0:T(8,128)(2,1)} %convolution_convert_fusion.1), kind=kCustom, calls=%all-reduce-scatter.1 | all-reduce-scatter fusion | flops 2621441 | bytes 4489728
  877.3 3.0 collective-permute-start.7
  880.3 2.2 collective-permute-start.6
  883.1 1.9 collective-permute-done.10
  887.9 6.4 concatenate.46
  896.3 45.3 %all-gather.5 = bf16[128,1,2048]{2,1,0:T(2,128)(2,1)S(1)} all-gather(bf16[1,1,2048]{2,1,0:T(2,128)(2,1)S(1)} %slice_bitcast_fusion.3), channel_id=1, replica_groups=mesh['dp'=4,'tensor'=32] {'dp','tensor'}, dimensions={0}, use_global_device_ids=true | all-gather | bytes 528384 | tf_op jit(solution)/shard_map/all_gather | solution.py:236
  (235 shorter events, 63.8 us)
Async XLA Ops:
  7.2 779.2 %copy-start = (bf16[2,2048,256]{2,1,0:T(8,128)(2,1)S(1)}, bf16[2,2048,256]{2,1,0:T(8,128)(2,1)}, u32[]{:S(2)}) copy-start(bf16[2,2048,256]{2,1,0:T(8,128)(2,1)} %param.19) | copy-start | bytes 6291460
  7.2 54.9 %all-gather.18.cloned.1.call-start = ((), (), s32[]{:S(2)}) async-start(), calls=%async_computation.7 | async-start | bytes 5406720 | tf_op jit(solution)/shard_map/all_gather | solution.py:64
  9.0 58.6 %copy-start.41 = (bf16[3,2048,64]{1,2,0:T(8,128)(2,1)S(1)}, bf16[3,2048,64]{1,2,0:T(8,128)(2,1)}, u32[]{:S(2)}) copy-start(bf16[3,2048,64]{1,2,0:T(8,128)(2,1)} %param.17) | copy-start | bytes 2359300
  9.0 109.9 %all-gather.14.cloned.1.call-start = ((), (), s32[]{:S(2)}) async-start(), calls=%async_computation.5 | async-start | bytes 4866048 | tf_op jit(solution)/shard_map/all_gather | solution.py:123
  67.6 5.7 copy-start.38
  67.6 5.7 copy-start.39
  67.6 6.4 copy-start.42
  67.6 6.7 copy-start.36
  72.5 95.0 %all-gather.12.cloned.1.call-start = ((), (), s32[]{:S(2)}) async-start(), calls=%async_computation.4 | async-start | bytes 4866048 | tf_op jit(solution)/shard_map/all_gather | solution.py:122
  73.2 143.2 %all-gather.16.cloned.1.call-start = ((), (), s32[]{:S(2)}) async-start(), calls=%async_computation.6 | async-start | bytes 4866048 | tf_op jit(solution)/shard_map/all_gather | solution.py:124
  89.1 8.1 slice-start
  89.1 8.1 slice-start.1
  127.4 0.7 copy-start.11
  128.1 45.9 %copy-start.33 = (bf16[1,16,64,2]{2,1,3,0:T(8,128)(2,1)}, bf16[1,16,64,2]{2,1,3,0:T(8,128)(2,1)S(1)}, u32[]{:S(2)}) copy-start(bf16[1,16,64,2]{2,1,3,0:T(8,128)(2,1)S(1)} %pad_maximum_fusion.7) | copy-start | bytes 12292
  199.4 20.5 %copy-start.4 = (bf16[32,16,64,2]{2,1,3,0:T(8,128)(2,1)}, bf16[32,16,64,2]{2,1,3,0:T(8,128)(2,1)S(1)}, u32[]{:S(2)}) copy-start(bf16[32,16,64,2]{2,1,3,0:T(8,128)(2,1)S(1)} %fusion.34) | copy-start | bytes 393220
  219.8 68.6 %copy-start.13 = (bf16[32,1,2048]{2,0,1:T(8,128)(2,1)}, bf16[32,1,2048]{2,0,1:T(8,128)(2,1)S(1)}, u32[]{:S(2)}) copy-start(bf16[32,1,2048]{2,0,1:T(8,128)(2,1)S(1)} %copy.220) | copy-start | bytes 393220
  338.7 5.8 copy-start.16
  338.7 5.8 copy-start.17
  371.0 8.0 copy-start.3
  379.0 3.6 copy-start.1
  379.0 3.6 copy-start.9
  382.6 1.6 copy-start.18
  384.9 10.4 %copy-start.21 = (bf16[32,16,48,1]{2,3,1,0:T(2,128)(2,1)S(1)}, bf16[32,16,48,1]{2,3,1,0:T(2,128)(2,1)}, u32[]{:S(2)}) copy-start(bf16[32,16,48,1]{2,3,1,0:T(2,128)(2,1)} %copy.260) | copy-start | bytes 147460
  389.1 48.9 %all-to-all-start.1 = ((f32[32,1,528]{2,1,0:T(1,128)}), f32[32,1,528]{2,1,0:T(1,128)S(1)}, u32[]{:S(2)}, u32[]{:S(2)}) async-start(f32[32,1,528]{2,1,0:T(1,128)} %reshape.604), calls=%async_computation.1 | async-start | bytes 163840 | tf_op jit(solution)/shard_map/all_to_all | solution.py:213
  395.3 4.7 copy-start.2
  400.0 1.3 copy-start.8
  438.0 16.2 %all-to-all-start.2 = ((f32[32,1,528]{2,1,0:T(1,128)}), f32[32,1,528]{2,1,0:T(1,128)S(1)}, u32[]{:S(2)}, u32[]{:S(2)}) async-start(f32[32,1,528]{2,1,0:T(1,128)} %reshape.606), calls=%async_computation.2 | async-start | bytes 163840 | tf_op jit(solution)/shard_map/all_to_all | solution.py:214
  454.2 133.4 %all-to-all-start = ((f32[32,33,2048]{2,1,0:T(8,128)}), f32[32,33,2048]{2,1,0:T(8,128)}, u32[]{:S(2)}, u32[]{:S(2)}) async-start(f32[32,33,2048]{2,1,0:T(8,128)} %pad_maximum_fusion), calls=%async_computation | async-start | bytes 20971520 | tf_op jit(solution)/shard_map/all_to_all | solution.py:215
  461.7 319.1 %all-gather.20.cloned.1.call-start = ((), (), s32[]{:S(2)}) async-start(), calls=%async_computation.8 | async-start | bytes 5406720 | tf_op jit(solution)/shard_map/all_gather | solution.py:64
  602.7 19.5 %copy-start.20 = (bf16[64,2048]{1,0:T(8,128)(2,1)S(1)}, bf16[64,2048]{1,0:T(8,128)(2,1)}, u32[]{:S(2)}) copy-start(bf16[64,2048]{1,0:T(8,128)(2,1)} %param.18) | copy-start | bytes 786436
  625.5 85.9 %copy-start.37 = (u32[128]{0:T(128)S(1)}, u32[128]{0:T(128)}, u32[]{:S(2)}) copy-start(u32[128]{0:T(128)} %constant.109) | copy-start | bytes 1540
  625.5 99.1 %copy-start.31 = (bf16[1,2048]{1,0:T(2,128)(2,1)S(1)}, bf16[1,2048]{1,0:T(2,128)(2,1)}, u32[]{:S(2)}) copy-start(bf16[1,2048]{1,0:T(2,128)(2,1)} %param.12) | copy-start | bytes 12292
  625.5 99.1 %copy-start.32 = (f32[1,2048]{1,0:T(1,128)S(1)}, f32[1,2048]{1,0:T(1,128)}, u32[]{:S(2)}) copy-start(f32[1,2048]{1,0:T(1,128)} %get-tuple-element.53) | copy-start | bytes 24580
  625.5 104.2 %copy-start.5 = (bf16[32,16,64,2]{2,1,3,0:T(8,128)(2,1)S(1)}, bf16[32,16,64,2]{2,1,3,0:T(8,128)(2,1)}, u32[]{:S(2)}) copy-start(bf16[32,16,64,2]{2,1,3,0:T(8,128)(2,1)} %copy-done.4) | copy-start | bytes 393220
  701.1 13.5 %copy-start.15 = (bf16[40,2048]{1,0:T(8,128)(2,1)}, bf16[40,2048]{1,0:T(8,128)(2,1)S(1)}, u32[]{:S(2)}) copy-start(bf16[40,2048]{1,0:T(8,128)(2,1)S(1)} %fusion) | copy-start | bytes 491524
  701.1 7.8 collective-permute-start.5
  702.4 11.4 %collective-permute-start.4 = (bf16[40,2048]{1,0:T(8,128)(2,1)S(1)}, bf16[40,2048]{1,0:T(8,128)(2,1)S(1)}, u32[]{:S(2)}, u32[]{:S(2)}) collective-permute-start(bf16[40,2048]{1,0:T(8,128)(2,1)S(1)} %fusion), channel_id=1, source_target_pairs={{0,5},{1,6},{2,7},{3,8},{4,9},{5,10},{6,11},{7,12},{8,13},{9,14},{... | collective-permute-start | bytes 491528
  703.7 10.1 %collective-permute-start.3 = (bf16[40,2048]{1,0:T(8,128)(2,1)S(1)}, bf16[40,2048]{1,0:T(8,128)(2,1)S(1)}, u32[]{:S(2)}, u32[]{:S(2)}) collective-permute-start(bf16[40,2048]{1,0:T(8,128)(2,1)S(1)} %fusion), channel_id=1, source_target_pairs={{0,4},{1,5},{2,6},{3,7},{4,8},{5,9},{6,10},{7,11},{8,12},{9,13},{1... | collective-permute-start | bytes 491528
  705.0 8.8 collective-permute-start.2
  706.3 8.2 collective-permute-start.1
  709.0 9.1 collective-permute-start
  713.8 0.8 copy-start.22
  713.8 0.8 copy-start.23
  713.8 0.8 copy-start.24
  714.6 0.7 copy-start.26
  724.4 5.3 copy-start.6
  786.3 4.7 copy-start.40
  794.4 77.4 %copy-start.14 = (bf16[32,1,2048]{2,0,1:T(8,128)(2,1)S(1)}, bf16[32,1,2048]{2,0,1:T(8,128)(2,1)}, u32[]{:S(2)}) copy-start(bf16[32,1,2048]{2,0,1:T(8,128)(2,1)} %copy-done.13) | copy-start | bytes 393220
  794.4 77.4 %copy-start.19 = (bf16[1,2,16,2048]{3,2,1,0:T(8,128)(2,1)S(1)}, bf16[1,2,16,2048]{3,2,1,0:T(8,128)(2,1)}, u32[]{:S(2)}) copy-start(bf16[1,2,16,2048]{3,2,1,0:T(8,128)(2,1)} %copy.246) | copy-start | bytes 393220
  794.4 78.1 %copy-start.34 = (bf16[1,16,64,2]{2,1,3,0:T(8,128)(2,1)S(1)}, bf16[1,16,64,2]{2,1,3,0:T(8,128)(2,1)}, u32[]{:S(2)}) copy-start(bf16[1,16,64,2]{2,1,3,0:T(8,128)(2,1)} %copy-done.33) | copy-start | bytes 12292
  794.4 78.7 %copy-start.7 = (bf16[1,1,2048]{0,2,1:T(8,128)(2,1)S(1)}, bf16[1,1,2048]{0,2,1:T(8,128)(2,1)}, u32[]{:S(2)}) copy-start(bf16[1,1,2048]{0,2,1:T(8,128)(2,1)} %get-tuple-element.30) | copy-start | bytes 12292
  794.4 100.1 %copy-start.12 = (bf16[2,16,2048]{2,1,0:T(8,128)(2,1)S(1)}, bf16[2,16,2048]{2,1,0:T(8,128)(2,1)}, u32[]{:S(2)}) copy-start(bf16[2,16,2048]{2,1,0:T(8,128)(2,1)} %param.11) | copy-start | bytes 393220
  794.4 100.1 %copy-start.35 = (f32[1,2048]{1,0:T(1,128)S(1)}, f32[1,2048]{1,0:T(1,128)}, u32[]{:S(2)}) copy-start(f32[1,2048]{1,0:T(1,128)} %get-tuple-element.52) | copy-start | bytes 24580
  870.5 9.7 %collective-permute-start.11 = (bf16[17,2048]{1,0:T(8,128)(2,1)S(1)}, bf16[17,2048]{1,0:T(8,128)(2,1)S(1)}, u32[]{:S(2)}, u32[]{:S(2)}) collective-permute-start(bf16[17,2048]{1,0:T(8,128)(2,1)S(1)} %slice.165), channel_id=1, source_target_pairs={{0,6},{1,7},{2,8},{3,9},{4,10},{5,11},{6,12},{7,13},{8,14},{9,15},... | collective-permute-start | bytes 208904
  873.3 11.7 %collective-permute-start.10 = (bf16[40,2048]{1,0:T(8,128)(2,1)S(1)}, bf16[40,2048]{1,0:T(8,128)(2,1)S(1)}, u32[]{:S(2)}, u32[]{:S(2)}) collective-permute-start(bf16[40,2048]{1,0:T(8,128)(2,1)S(1)} %fusion.1), channel_id=1, source_target_pairs={{0,5},{1,6},{2,7},{3,8},{4,9},{5,10},{6,11},{7,12},{8,13},{9,14},{... | collective-permute-start | bytes 491528
  874.6 10.4 %collective-permute-start.9 = (bf16[40,2048]{1,0:T(8,128)(2,1)S(1)}, bf16[40,2048]{1,0:T(8,128)(2,1)S(1)}, u32[]{:S(2)}, u32[]{:S(2)}) collective-permute-start(bf16[40,2048]{1,0:T(8,128)(2,1)S(1)} %fusion.1), channel_id=1, source_target_pairs={{0,4},{1,5},{2,6},{3,7},{4,8},{5,9},{6,10},{7,11},{8,12},{9,13},{1... | collective-permute-start | bytes 491528
  875.9 9.1 collective-permute-start.8
  877.3 7.8 collective-permute-start.7
  880.3 4.8 copy-start.30
  880.3 7.6 collective-permute-start.6
  885.0 0.7 copy-start.25
  885.0 0.7 copy-start.27
  885.0 0.8 copy-start.28
  885.8 0.7 copy-start.29
  (1 other events, 0.6 us)
Sparse Core Ops, SparseCore 0:
  10.8 51.1 all-gather.17
  72.6 46.2 all-gather.13
  121.1 46.2 all-gather.11
  170.1 46.2 all-gather.15
  726.6 54.0 all-gather.19
where the time goes:
time: 955 us; the launch traced here: 949 us
  waiting for transfers between devices  288 us (30%)
  local copies, waits for them, and re-layouts  268 us (28%)
  blocking collectives  215 us (23%)
  other arithmetic  87.8 us (9%)
  starting transfers between devices  41.4 us (4%)
  matrix products  32 us (3%)
  between operations  17.6 us (2%)
    unnamed x2, blocking collectives  152 us
    all_to_all x1, waiting for transfers between devices, local(): lax.all_to_all(mixed, 'tensor', split_axis=0, concat_axis=0, tiled=True)  123 us
    convert_element_type x2, local copies, waits for them, and re-layouts, local(): query_prompt.astype(jnp.float32)  112 us
    all_gather x2, waiting for transfers between devices, spread(): lax.all_gather(local_rows, 'tensor', axis=0, tiled=True)  98.2 us
    unnamed x114, local copies, waits for them, and re-layouts  47.6 us
    all_gather x1, blocking collectives, local(): lax.all_gather(output[prompt_own:], ('dp', 'tensor'), axis=0, tiled=True)  45.3 us
    all_gather x1, waiting for transfers between devices, local(): lax.all_gather(query_raw, 'tensor', axis=1, tiled=True)  38.5 us
    unnamed x12, starting transfers between devices  20.6 us
  transfers between devices with their start and end apart: 20, of which 11 were waited for; matrix products, arithmetic and copies ran while one was open for 16% of the time, Pallas kernels for 0%

commit v1 on v0

v1 whole, which is shorter than its diff:
```python
import jax
import jax.numpy as jnp
import numpy as np
from jax import lax
from jax.experimental import pallas as pl
from jax.experimental.pallas import tpu as pltpu
from jax.sharding import PartitionSpec as P

D = 2048
HD = 128
HEADS = 16
FFD = 256
CTX = 48
ROWS = 528
EPSILON = 1e-06
ROPE_BASE = 500000.0
MASKED_SCORE = -1e30
SCALE = HD ** (-0.5)
BF = jnp.bfloat16
F32 = jnp.float32
MESH = pl.DeviceIdType.MESH
NT = (((1,), (1,)), ((), ()))


def mul(value, factor):
    return pl.multiple_of(value * factor, factor)


def remote(src, dst, send_sem, recv_sem, dev):
    return pltpu.make_async_remote_copy(
        src_ref=src,
        dst_ref=dst,
        send_sem=send_sem,
        recv_sem=recv_sem,
        device_id={"tensor": dev},
        device_id_type=MESH,
    )


class Plane:
    def __init__(self):
        self.y = lax.axis_index("dp")
        self.t = lax.axis_index("tensor")
        self.c = lax.rem(self.t, 2)
        self.q = lax.div(self.t, 2)
        x = lax.rem(self.q, 4)
        z = lax.div(self.q, 4)
        self.a = x + self.c * (z - x)
        self.b = z + self.c * (x - z)
        self.sib = self.t + 1 - 2 * self.c
        self.aR, self.aO, self.aL = [lax.rem(self.a + i, 4) for i in (1, 2, 3)]
        self.bR, self.bO, self.bL = [lax.rem(self.b + i, 4) for i in (1, 2, 3)]

    def chip(self, a, b):
        return a * (1 + 3 * self.c) + b * (4 - 3 * self.c)

    def dev(self, a, b):
        return 2 * self.chip(a, b) + self.c


def block(buf, chip):
    return buf.at[pl.ds(mul(chip, 32), 32)]


def half(buf, chip, h):
    return buf.at[pl.ds(mul(chip * 2 + h, 16), 16)]


def gather_steps(p, buf, ss, rs, sends):
    def send(slot, ref, dev):
        copy = remote(ref, ref, ss.at[slot], rs.at[slot], dev)
        copy.start()
        sends.append(copy)

    def recv(slot, ref):
        remote(ref, ref, ss.at[slot], rs.at[slot], p.dev(p.aR, p.b)).wait_recv()

    def blk(a, b):
        return block(buf, p.chip(a, b))

    def hlf(a, b, h):
        return half(buf, p.chip(a, b), h)

    a, b, aR, aL, aO, bR, bL, bO = p.a, p.b, p.aR, p.aL, p.aO, p.bR, p.bL, p.bO
    to_aR, to_aL, to_bR, to_bL = p.dev(aR, b), p.dev(aL, b), p.dev(a, bR), p.dev(a, bL)
    own = blk(a, b)
    send(0, own, to_aR)
    send(1, own, to_aL)
    send(4, own, to_bR)
    send(5, own, to_bL)
    yield
    recv(0, blk(aL, b))
    send(2, hlf(aL, b, 0), to_aR)
    send(8, blk(aL, b), to_bR)
    send(9, blk(aL, b), to_bL)
    recv(1, blk(aR, b))
    send(3, hlf(aR, b, 1), to_aL)
    send(12, blk(aR, b), to_bR)
    send(13, blk(aR, b), to_bL)
    yield
    recv(4, blk(a, bL))
    send(6, hlf(a, bL, 0), to_bR)
    recv(5, blk(a, bR))
    send(7, hlf(a, bR, 1), to_bL)
    yield
    recv(2, hlf(aO, b, 0))
    recv(3, hlf(aO, b, 1))
    send(16, blk(aO, b), to_bR)
    send(17, blk(aO, b), to_bL)
    yield
    for k, ak in ((1, aL), (2, aR), (3, aO)):
        recv(4 + 4 * k, blk(ak, bL))
        send(6 + 4 * k, hlf(ak, bL, 0), to_bR)
        recv(5 + 4 * k, blk(ak, bR))
        send(7 + 4 * k, hlf(ak, bR, 1), to_bL)
        yield
    for k, ak in ((0, a), (1, aL), (2, aR), (3, aO)):
        recv(6 + 4 * k, hlf(ak, bO, 0))
        recv(7 + 4 * k, hlf(ak, bO, 1))
        yield


def reduce_rows(p, buf, land, ss, rs, sends):
    def send(slot, ref, dev):
        copy = remote(ref, land.at[slot], ss.at[slot], rs.at[slot], dev)
        copy.start()
        sends.append(copy)

    def recv(slot):
        remote(land.at[slot], land.at[slot], ss.at[slot], rs.at[slot], p.dev(p.aR, p.b)).wait_recv()
        return land[slot].astype(F32)

    def hlf(a, b, h):
        return half(buf, p.chip(a, b), h)

    def add(ref, slots):
        total = ref[...].astype(F32)
        for slot in slots:
            total = total + recv(slot)
        return total

    a, b, aR, aL, aO, bR, bL, bO = p.a, p.b, p.aR, p.aL, p.aO, p.bR, p.bL, p.bO
    to_aR, to_aL, to_bR, to_bL = p.dev(aR, b), p.dev(aL, b), p.dev(a, bR), p.dev(a, bL)
    order = ((3, aO), (1, aL), (2, aR), (0, a))
    for k, ak in order:
        send(6 * k + 0, hlf(ak, bO, 0), to_bL)
        send(6 * k + 1, hlf(ak, bO, 1), to_bR)
        send(6 * k + 2, hlf(ak, bL, 1), to_bL)
        send(6 * k + 3, hlf(ak, bR, 0), to_bR)
    for k, ak in order:
        ref = hlf(ak, bL, 0)
        ref[...] = add(ref, (6 * k + 0,)).astype(BF)
        send(6 * k + 4, ref, to_bL)
        ref = hlf(ak, bR, 1)
        ref[...] = add(ref, (6 * k + 1,)).astype(BF)
        send(6 * k + 5, ref, to_bR)
    for k, ak in order:
        h0, h1 = hlf(ak, b, 0), hlf(ak, b, 1)
        h0[...] = add(h0, (6 * k + 3, 6 * k + 4)).astype(BF)
        h1[...] = add(h1, (6 * k + 2, 6 * k + 5)).astype(BF)
        if k == 3:
            send(24, h0, to_aL)
            send(25, h1, to_aR)
        if k == 1:
            send(26, h1, to_aL)
        if k == 2:
            send(27, h0, to_aR)
    ref = hlf(aL, b, 0)
    ref[...] = add(ref, (24,)).astype(BF)
    send(28, ref, to_aL)
    ref = hlf(aR, b, 1)
    ref[...] = add(ref, (25,)).astype(BF)
    send(29, ref, to_aR)
    first = add(hlf(a, b, 0), (27, 28))
    second = add(hlf(a, b, 1), (26, 29))
    return jnp.concatenate([first, second], axis=0)


def turn(values, cosine, sine):
    lane = lax.broadcasted_iota(jnp.int32, values.shape, 1)
    swapped = jnp.where(lane % 2 == 0, pltpu.roll(values, HD - 1, 1), pltpu.roll(values, 1, 1))
    return values * cosine + swapped * sine


def angles(positions, freq):
    turned = positions * freq
    lane = lax.broadcasted_iota(jnp.int32, turned.shape, 1)
    return jnp.cos(turned), jnp.where(lane % 2 == 0, -1.0, 1.0) * jnp.sin(turned)


def kernel(
    prompt_states,
    decode_states,
    cache,
    prompt_starts,
    lengths,
    slots_row,
    slots,
    w_qkv,
    w_out,
    w_gate_up,
    w_down,
    gains,
    freq,
    prompt_out,
    decode_out,
    new_prompt_kv,
    new_decode_kv,
    X1,
    X2,
    Y,
    Y2,
    RB1,
    RB2,
    WQ,
    WO,
    WG,
    WD,
    KD,
    VD,
    CK,
    QR,
    KN,
    NKV,
    ATT,
    ACT,
    SS,
    DX,
    XD,
    DQ,
    DKV,
    QH,
    KH,
    LEN,
    DCS,
    OBF,
    OB,
    SB,
    OR,
    SR,
    DY,
    DR,
    DX2,
    DY2,
    DR2,
    PO,
    FIN,
    FS,
    FD,
    g1s,
    g1r,
    g2s,
    g2r,
    r1s,
    r1r,
    r2s,
    r2r,
    ws,
    wr,
    wl,
    ls,
    ms,
    mr,
    ys,
    yr,
):
    p = Plane()
    y, t, c, q, sib = p.y, p.t, p.c, p.q, p.sib
    sends = []
    lanes_q = pl.ds(mul(q, HD), HD)

    barrier = pltpu.get_barrier_semaphore()

    @pl.loop(1, 32)
    def _(i):
        pl.semaphore_signal(
            barrier, inc=1, device_id={"tensor": lax.rem(t + i, 32)}, device_id_type=MESH
        )

    for i in (1, 2, 3):
        pl.semaphore_signal(barrier, inc=1, device_id={"dp": lax.rem(y + i, 4)}, device_id_type=MESH)
    pl.semaphore_wait(barrier, 34)

    def plane_peers(body):
        @pl.loop(1, 16)
        def _(i):
            chip = lax.rem(q + i, 16)
            body(chip, 2 * chip + c)

    def group_peers(body):
        @pl.loop(1, 32)
        def _(i):
            body(lax.rem(t + i, 32))

    def drain_recv(ref, sem):
        remote(ref, ref, sem, sem, sib).wait_recv()

    def drain_send(ref, sem):
        remote(ref, ref, sem, sem, sib).wait_send()

    for j in range(HEADS):
        DX[q, pl.ds(j, 1), :] = decode_states[:, j * HD : (j + 1) * HD].astype(F32)
    plane_peers(lambda chip, dev: remote(DX.at[q], DX.at[q], ms.at[0], mr.at[0], dev).start())

    piece = remote(
        prompt_states.at[1 - c], half(X1, q, c), ws.at[0], wr.at[0], sib
    )
    piece.start()
    piece_here = pltpu.make_async_copy(prompt_states.at[c], half(X1, q, c), wl.at[0])
    piece_here.start()
    weights = []
    for i, (src, dst) in enumerate(
        (
            (w_qkv, WQ.at[:, c]),
            (w_out, WO.at[c]),
            (w_gate_up, WG.at[c]),
            (w_down, WD.at[c]),
        )
    ):
        here = pltpu.make_async_copy(src, dst, wl.at[1 + i])
        there = remote(src, dst, ws.at[1 + i], wr.at[1 + i], sib)
        here.start()
        there.start()
        weights.append((here, there))

    def weight_here(i):
        here, there = weights[i]
        here.wait()
        there.wait_recv()

    loads = []
    for i, (kv, dst) in enumerate(((0, KD), (1, VD))):
        for part in range(2):
            load = pltpu.make_async_copy(
                cache.at[kv, pl.ds(2 + 16 * part, 16)], dst.at[pl.ds(16 * part, 16)], ls.at[2 * i + part]
            )
            load.start()
            loads.append(load)

    piece_here.wait()
    piece.wait_recv()
    steps = gather_steps(p, X1, g1s, g1r, sends)
    next(steps)

    def cache_slice(dev):
        return cache.at[:, lax.rem(dev, 2), :, pl.ds(mul(lax.div(dev, 2), HD), HD)]

    own_cache = pltpu.make_async_copy(cache_slice(t), CK.at[:, t], wl.at[5])
    own_cache.start()
    group_peers(
        lambda dev: remote(cache_slice(dev), CK.at[:, t], ms.at[1], mr.at[1], dev).start()
    )

    drain_recv(DX.at[pl.ds(0, 15)], mr.at[0])
    for j in range(HEADS):
        XD[:, j * HD : (j + 1) * HD] = DX[:, j, :].astype(BF)
    weight_here(0)

    def project(rows):
        return lax.dot_general(rows, WQ[...].reshape(3 * HD, D), NT, preferred_element_type=F32)

    dec = project(XD[...]).astype(BF)
    DQ[c, :, lanes_q] = dec[:, :HD]
    DKV[0, :, lanes_q] = dec[:, HD : 2 * HD]
    DKV[1, :, lanes_q] = dec[:, 2 * HD :]
    q_own = DQ.at[c, :, lanes_q]
    kv_own = DKV.at[:, :, lanes_q]
    group_peers(lambda dev: remote(q_own, q_own, ms.at[2], mr.at[2], dev).start())
    plane_peers(lambda chip, dev: remote(kv_own, kv_own, ms.at[3], mr.at[3], dev).start())
    next(steps)

    slot_row = lax.broadcasted_iota(jnp.int32, (32, HD), 0)
    slot_id = 32 * y + 2 * (slot_row % 16) + slot_row // 16
    matched = jnp.where(slots_row[...] == slot_id, lengths[...].astype(F32), 0.0)
    slot_len = jnp.sum(matched, axis=1, keepdims=True)
    LEN[...] = jnp.broadcast_to(slot_len, (32, HD))
    cosine, sine = angles(LEN[...], freq[...])
    DCS[0] = cosine
    DCS[1] = sine
    next(steps)

    drain_recv(OR.at[pl.ds(0, 31)], mr.at[2])
    drain_recv(KN.at[:, pl.ds(0, 240)], mr.at[3])

    def normed(raw, gain_row, first):
        scale = lax.rsqrt(jnp.mean(raw * raw, axis=1, keepdims=True) + EPSILON)
        rows = raw.shape[0]
        cos_part, sin_part = DCS[0, pl.ds(first, rows), :], DCS[1, pl.ds(first, rows), :]
        parts = []
        for j in range(HEADS):
            lanes = slice(j * HD, (j + 1) * HD)
            scaled = raw[:, lanes] * scale * gains[gain_row : gain_row + 1, lanes]
            parts.append(turn(scaled, cos_part, sin_part).astype(BF).astype(F32))
        return parts

    for plane in range(2):
        for j, part in enumerate(normed(DQ[plane].astype(F32), 0, 16 * plane)):
            QH[16 * plane : 16 * plane + 16, j * HD : (j + 1) * HD] = part
    for j, part in enumerate(normed(DKV[0].astype(F32), 1, mul(c, 16))):
        KH[:, j * HD : (j + 1) * HD] = part
    for load in loads:
        load.wait()

    own_lane = lax.broadcasted_iota(jnp.int32, (HEADS, D), 1) // HD
    own_row = lax.broadcasted_iota(jnp.int32, (HEADS, D), 0)
    own_head = own_lane == own_row
    spot = (lax.broadcasted_iota(jnp.int32, (HEADS, CTX), 1) + CTX * t).astype(F32)
    low_lane = lax.broadcasted_iota(jnp.int32, (HEADS, HD), 1) < 64

    def decode_slots_from(first, count):
        @pl.loop(first, first + count)
        def _(s):
            plane = lax.rem(s, 2)
            r = lax.div(s, 2)
            index = 16 * plane + r
            spread = jnp.where(own_head, QH[pl.ds(index, 1), :], 0.0).astype(BF)
            scores = lax.dot_general(spread, KD[s], NT, preferred_element_type=F32) * SCALE
            live = spot < LEN[pl.ds(index, 1), :CTX]
            scores = jnp.where(live, scores, MASKED_SCORE)
            top = jnp.max(scores, axis=1, keepdims=True)
            probs = jnp.where(live, jnp.exp(scores - top), 0.0)
            total = jnp.sum(probs, axis=1, keepdims=True)
            mixed = jnp.dot(probs.astype(BF), VD[s], preferred_element_type=F32)
            OBF[pl.ds(index, 1), :] = jnp.sum(jnp.where(own_head, mixed, 0.0), axis=0, keepdims=True)
            SB[plane, :, r, :] = jnp.where(low_lane, top, total)

    done = 0
    for _ in steps:
        if done < 32:
            decode_slots_from(done, 4)
            done += 4
    if done < 32:
        decode_slots_from(done, 32 - done)

    OB[0] = OBF[0:16, :].astype(BF)
    OB[1] = OBF[16:32, :].astype(BF)

    def mixed_slice(dev):
        return OB.at[lax.rem(dev, 2), :, pl.ds(mul(lax.div(dev, 2), HD), HD)]

    def stat_slice(dev):
        return SB.at[lax.rem(dev, 2), lax.div(dev, 2)]

    own_mixed = pltpu.make_async_copy(mixed_slice(t), OR.at[t], wl.at[6])
    own_stat = pltpu.make_async_copy(stat_slice(t), SR.at[t], wl.at[7])
    own_mixed.start()
    own_stat.start()

    def send_partial(dev):
        remote(mixed_slice(dev), OR.at[t], ms.at[4], mr.at[4], dev).start()
        remote(stat_slice(dev), SR.at[t], ms.at[5], mr.at[5], dev).start()

    group_peers(send_partial)

    stat_row = lax.broadcasted_iota(jnp.int32, (8, HD), 0)
    SS[q] = jnp.zeros((8, HD), F32)

    def row_sums(values):
        total = jnp.sum(values * values, axis=1, keepdims=True)
        return jnp.broadcast_to(total, (HD, HD)).T[0:8, :]

    @pl.loop(0, 4)
    def _(i):
        rows = pl.ds(mul(i, HD), HD)
        got = project(X1[rows, :])
        query = got[:, :HD].astype(BF)
        key = got[:, HD : 2 * HD].astype(BF)
        QR[rows, :] = query
        KN[0, rows, :] = key
        KN[1, rows, :] = got[:, 2 * HD :].astype(BF)
        query_sum = row_sums(query.astype(F32))
        key_sum = row_sums(key.astype(F32))
        SS[q] = jnp.where(
            stat_row == i, query_sum, jnp.where(stat_row == 4 + i, key_sum, SS[q])
        )

    plane_peers(lambda chip, dev: remote(SS.at[q], SS.at[q], ms.at[6], mr.at[6], dev).start())
    drain_recv(SS.at[pl.ds(0, 15)], mr.at[6])
    sums = jnp.sum(SS[...], axis=0)
    scales = lax.rsqrt(sums * (1.0 / D) + EPSILON)
    start = prompt_starts[2 * y + c]

    for i in range(4):
        rows = slice(i * HD, (i + 1) * HD)
        offset = lax.broadcasted_iota(jnp.int32, (HD, HD), 0) + i * HD
        cosine, sine = angles((offset + start).astype(F32), freq[...])
        for kind in range(2):
            column = jnp.broadcast_to(scales[4 * kind + i : 4 * kind + i + 1, :], (HD, HD)).T
            raw = (QR[rows, :] if kind == 0 else KN[0, rows, :]).astype(F32)
            turned = turn(raw * column * gains[kind : kind + 1, lanes_q], cosine, sine).astype(BF)
            if kind == 0:
                QR[rows, :] = turned
            else:
                KN[0, rows, :] = turned

    def fresh_slice(dev):
        return KN.at[:, pl.ds(mul(dev, 16), 16), :]

    landing = NKV.at[:, c, :, lanes_q]
    own_fresh = pltpu.make_async_copy(fresh_slice(t), landing, wl.at[8])
    own_fresh.start()
    group_peers(lambda dev: remote(fresh_slice(dev), landing, ms.at[7], mr.at[7], dev).start())

    own_cache.wait()
    drain_recv(CK.at[:, pl.ds(0, 31)], mr.at[1])

    @pl.loop(0, 4)
    def _(i):
        rows = pl.ds(mul(i, HD), HD)
        query = QR[rows, :]
        cached_keys = CK[0].reshape(32 * CTX, HD)
        cached_values = CK[1].reshape(32 * CTX, HD)
        fresh = lax.dot_general(query, KN[0], NT, preferred_element_type=F32) * SCALE
        cached = lax.dot_general(query, cached_keys, NT, preferred_element_type=F32) * SCALE
        column = lax.broadcasted_iota(jnp.int32, fresh.shape, 1)
        row = lax.broadcasted_iota(jnp.int32, fresh.shape, 0) + i * HD
        fresh_live = column <= row
        cached_live = lax.broadcasted_iota(jnp.int32, cached.shape, 1) < start
        fresh = jnp.where(fresh_live, fresh, MASKED_SCORE)
        cached = jnp.where(cached_live, cached, MASKED_SCORE)
        top = jnp.maximum(
            jnp.max(fresh, axis=1, keepdims=True), jnp.max(cached, axis=1, keepdims=True)
        )
        fresh = jnp.where(fresh_live, jnp.exp(fresh - top), 0.0)
        cached = jnp.where(cached_live, jnp.exp(cached - top), 0.0)
        total = jnp.sum(fresh, axis=1, keepdims=True) + jnp.sum(cached, axis=1, keepdims=True)
        mixed = jnp.dot(fresh.astype(BF), KN[1], preferred_element_type=F32)
        mixed = mixed + jnp.dot(cached.astype(BF), cached_values, preferred_element_type=F32)
        ATT[rows, :] = (mixed / total).astype(BF)

    own_mixed.wait()
    own_stat.wait()
    drain_recv(OR.at[pl.ds(0, 31)], mr.at[4])
    drain_recv(SR.at[pl.ds(0, 31)], mr.at[5])
    stats = SR[...].reshape(32 * 16, HD)
    rolled = pltpu.roll(stats, 64, 1)
    low = lax.broadcasted_iota(jnp.int32, stats.shape, 1) < 64
    tops = jnp.where(low, stats, rolled).reshape(32, 16, HD)
    totals = jnp.where(low, rolled, stats).reshape(32, 16, HD)
    own_rows = pl.ds(mul(c, 16), 16)
    own_score = (
        jnp.sum(QH[own_rows, lanes_q] * KH[:, lanes_q], axis=1, keepdims=True) * SCALE
    )
    highest = jnp.maximum(jnp.max(tops, axis=0), own_score)
    factors = jnp.exp(tops - highest[None])
    own_weight = jnp.exp(own_score - highest)
    total = jnp.sum(totals * factors, axis=0) + own_weight
    mixed = jnp.sum(OR[...].astype(F32) * factors, axis=0)
    mixed = mixed + own_weight.astype(BF).astype(F32) * DKV[1, :, lanes_q].astype(F32)
    ATT[512:528, :] = (mixed / total).astype(BF)

    weight_here(1)

    @pl.loop(0, 3)
    def _(i):
        rows = pl.ds(mul(i, 176), 176)
        Y[rows, :] = jnp.dot(
            ATT[rows, :], WO[...].reshape(HD, D), preferred_element_type=F32
        ).astype(BF)

    def spread_decode(source, staged, landed, index):
        tail = source[512:528, :].astype(F32)
        for j in range(HEADS):
            staged[:, j, :] = tail[:, j * HD : (j + 1) * HD]
        landed[q] = staged[q]
        plane_peers(
            lambda chip, dev: remote(
                staged.at[chip], landed.at[q], ms.at[index], mr.at[index], dev
            ).start()
        )

    def row_of(gain):
        parts = [gains[gain : gain + 1, j * HD : (j + 1) * HD] for j in range(HEADS)]
        return jnp.concatenate(parts, axis=0)

    def add_normed_rows(base, total, gain):
        scale = lax.rsqrt(jnp.mean(total * total, axis=1, keepdims=True) + EPSILON)
        return (base + total * scale * gains[gain : gain + 1, :]).astype(BF)

    def add_normed_row(base, total, gain):
        square = jnp.sum(total * total, axis=1, keepdims=True)
        mean = jnp.sum(square, axis=0, keepdims=True) * (1.0 / D)
        return (base + total * lax.rsqrt(mean + EPSILON) * row_of(gain)).astype(BF).astype(F32)

    own_block = pl.ds(mul(q, 32), 32)
    spread_decode(Y, DY, DR, 8)
    attn_rows = reduce_rows(p, Y, RB1, r1s, r1r, sends)
    X2[own_block, :] = add_normed_rows(X1[own_block, :].astype(F32), attn_rows, 2)
    steps = gather_steps(p, X2, g2s, g2r, sends)
    next(steps)
    drain_recv(DR.at[pl.ds(0, 15)], mr.at[8])
    DX2[q] = add_normed_row(DX[q], jnp.sum(DR[...], axis=0), 2)
    plane_peers(lambda chip, dev: remote(DX2.at[q], DX2.at[q], ms.at[9], mr.at[9], dev).start())
    for _ in steps:
        pass
    drain_recv(DX2.at[pl.ds(0, 15)], mr.at[9])
    for j in range(HEADS):
        X2[512:528, j * HD : (j + 1) * HD] = DX2[:, j, :].astype(BF)

    weight_here(2)
    weight_here(3)

    @pl.loop(0, 3)
    def _(i):
        rows = pl.ds(mul(i, 176), 176)
        hidden = X2[rows, :]
        for core in range(2):
            gate = jnp.dot(hidden, WG[core, 0], preferred_element_type=F32)
            up = jnp.dot(hidden, WG[core, 1], preferred_element_type=F32)
            ACT[core] = (gate / (1.0 + jnp.exp(-gate)) * up).astype(BF)
        Y2[rows, :] = (
            jnp.dot(ACT[0], WD[0], preferred_element_type=F32)
            + jnp.dot(ACT[1], WD[1], preferred_element_type=F32)
        ).astype(BF)

    spread_decode(Y2, DY2, DR2, 10)
    ffn_rows = reduce_rows(p, Y2, RB2, r2s, r2r, sends)
    out_rows = add_normed_rows(X2[own_block, :].astype(F32), ffn_rows, 3)
    FS[...] = out_rows.reshape(2, 16, D)
    PO[c] = FS[c]
    swap = remote(FS.at[1 - c], PO.at[c], ws.at[5], wr.at[5], sib)
    swap.start()

    drain_recv(DR2.at[pl.ds(0, 15)], mr.at[10])
    FIN[t] = add_normed_row(DX2[q], jnp.sum(DR2[...], axis=0), 3)
    group_peers(lambda dev: remote(FIN.at[t], FIN.at[t], ms.at[11], mr.at[11], dev).start())

    own_fresh.wait()
    drain_recv(KN.at[:, pl.ds(0, 496)], mr.at[7])
    new_prompt_kv[...] = NKV[...]
    mine = lax.broadcasted_iota(jnp.int32, (16, D), 0) == q
    new_decode_kv[0] = jnp.sum(jnp.where(mine, KH[...], 0.0), axis=0, keepdims=True).astype(BF)
    new_decode_kv[1] = jnp.sum(
        jnp.where(mine, DKV[1].astype(F32), 0.0), axis=0, keepdims=True
    ).astype(BF)

    drain_recv(FIN.at[pl.ds(0, 31)], mr.at[11])
    slot_of = lax.broadcasted_iota(jnp.int32, (32, 16, HD), 0) + 32 * y

    def wanted_row(yy):
        wanted = slots[32 * yy + t]
        return jnp.sum(jnp.where(slot_of == wanted, FIN[...], 0.0), axis=0)

    FD[0] = wanted_row(y)
    crossing = []
    for i in (1, 2, 3):
        other = lax.rem(y + i, 4)
        FD[3 + i] = wanted_row(other)
        copy = pltpu.make_async_remote_copy(
            src_ref=FD.at[3 + i],
            dst_ref=FD.at[i],
            send_sem=ys.at[i - 1],
            recv_sem=yr.at[i - 1],
            device_id={"dp": other},
            device_id_type=MESH,
        )
        copy.start()
        crossing.append(copy)
    swap.wait_recv()
    prompt_out[...] = PO[...]
    result = FD[0]
    for i, copy in enumerate(crossing):
        copy.wait_recv()
        result = result + FD[1 + i]
    for j in range(HEADS):
        decode_out[:, j * HD : (j + 1) * HD] = result[j : j + 1, :].astype(BF)

    for copy in sends + crossing + [piece, swap]:
        copy.wait_send()
    for _, there in weights:
        there.wait_send()
    drain_send(DX.at[pl.ds(0, 15)], ms.at[0])
    drain_send(CK.at[:, pl.ds(0, 31)], ms.at[1])
    drain_send(OR.at[pl.ds(0, 31)], ms.at[2])
    drain_send(KN.at[:, pl.ds(0, 240)], ms.at[3])
    drain_send(OR.at[pl.ds(0, 31)], ms.at[4])
    drain_send(SR.at[pl.ds(0, 31)], ms.at[5])
    drain_send(SS.at[pl.ds(0, 15)], ms.at[6])
    drain_send(KN.at[:, pl.ds(0, 496)], ms.at[7])
    drain_send(DR.at[pl.ds(0, 15)], ms.at[8])
    drain_send(DX2.at[pl.ds(0, 15)], ms.at[9])
    drain_send(DR2.at[pl.ds(0, 15)], ms.at[10])
    drain_send(FIN.at[pl.ds(0, 31)], ms.at[11])


def local(
    prompt_states,
    decode_states,
    cache,
    prompt_starts,
    decode_lengths,
    decode_slots,
    w_qkv,
    w_out,
    w_gate_up,
    w_down,
    gains,
):
    freq = np.power(ROPE_BASE, -2.0 * (np.arange(HD) // 2) / HD).astype(np.float32)[None, :]
    vmem = pl.BlockSpec(memory_space=pltpu.VMEM)
    smem = pl.BlockSpec(memory_space=pltpu.SMEM)
    hbm = pl.BlockSpec(memory_space=pl.ANY)
    scratch = [
        ((ROWS, D), BF),
        ((ROWS, D), BF),
        ((ROWS, D), BF),
        ((ROWS, D), BF),
        ((30, 16, D), BF),
        ((30, 16, D), BF),
        ((3, 2, 64, D), BF),
        ((2, 64, D), BF),
        ((2, 2, D, FFD), BF),
        ((2, FFD, D), BF),
        ((32, CTX, D), BF),
        ((32, CTX, D), BF),
        ((2, 32, CTX, HD), BF),
        ((512, HD), BF),
        ((2, 512, HD), BF),
        ((2, 2, 16, D), BF),
        ((ROWS, HD), BF),
        ((2, 176, FFD), BF),
        ((16, 8, HD), F32),
        ((16, 16, HD), F32),
        ((16, D), BF),
        ((2, 16, D), BF),
        ((2, 16, D), BF),
        ((32, D), F32),
        ((16, D), F32),
        ((32, HD), F32),
        ((2, 32, HD), F32),
        ((32, D), F32),
        ((2, 16, D), BF),
        ((2, 16, 16, HD), F32),
        ((32, 16, HD), BF),
        ((32, 16, HD), F32),
        ((16, 16, HD), F32),
        ((16, 16, HD), F32),
        ((16, 16, HD), F32),
        ((16, 16, HD), F32),
        ((16, 16, HD), F32),
        ((2, 16, D), BF),
        ((32, 16, HD), F32),
        ((2, 16, D), BF),
        ((7, 16, HD), F32),
    ]
    sems = [20, 20, 20, 20, 30, 30, 30, 30, 6, 6, 9, 4, 12, 12, 3, 3]
    outs = pl.pallas_call(
        kernel,
        out_shape=(
            jax.ShapeDtypeStruct((2, 16, D), BF),
            jax.ShapeDtypeStruct((1, D), BF),
            jax.ShapeDtypeStruct((2, 2, 16, D), BF),
            jax.ShapeDtypeStruct((2, 1, D), BF),
        ),
        in_specs=[hbm, vmem, hbm, smem, vmem, vmem, smem, hbm, hbm, hbm, hbm, vmem, vmem],
        out_specs=(vmem, vmem, vmem, vmem),
        scratch_shapes=[pltpu.VMEM(shape, dtype) for shape, dtype in scratch]
        + [pltpu.SemaphoreType.DMA((count,)) for count in sems],
        compiler_params=pltpu.CompilerParams(
            collective_id=0, has_side_effects=True, vmem_limit_bytes=60 * 1024 * 1024
        ),
        name="decoder_layer",
    )(
        prompt_states,
        decode_states,
        cache,
        prompt_starts,
        decode_lengths[None, :],
        decode_slots[None, :],
        decode_slots,
        jnp.swapaxes(w_qkv, 1, 2),
        w_out,
        w_gate_up,
        w_down,
        gains,
        jnp.asarray(freq),
    )
    return outs


def solution(mesh):
    in_specs = (
        P("dp", "tensor", None),
        P(("dp", "tensor"), None),
        P(None, "dp", "tensor", None),
        P(),
        P(),
        P(),
        P(None, None, "tensor"),
        P("tensor", None),
        P(None, None, "tensor"),
        P("tensor", None),
        P(),
    )
    out_specs = (
        P("dp", "tensor", None),
        P(("dp", "tensor"), None),
        P(None, "dp", "tensor", None),
        P(None, ("dp", "tensor"), None),
    )
    return jax.shard_map(local, mesh=mesh, in_specs=in_specs, out_specs=out_specs, check_vma=False)
```

time: 955 us -> 138 us (0.14)
  waiting for transfers between devices: 288 us -> 0 us
  local copies, waits for them, and re-layouts: 268 us -> 5.86 us
  blocking collectives: 215 us -> 0 us
  Pallas kernels: 0 us -> 131 us
  other arithmetic: 87.8 us -> 0 us
  starting transfers between devices: 41.4 us -> 0 us
  matrix products: 32 us -> 0 us
  between operations: 17.6 us -> 0.64 us
    all_gather x5 -> x0, waiting for transfers between devices: 156 us -> none  [the longest x2 98.2 us: spread(): lax.all_gather(local_rows, 'tensor', axis=0, tiled=True)]
    unnamed x2 -> x0, blocking collectives: 152 us -> none
    pallas_call x0 -> x1, Pallas kernels: none -> 131 us  [local(): pl.pallas_call(kernel, out_shape=(jax.ShapeDtypeStruct((2, 16, D), BF), j...]
    all_to_all x3 -> x0, waiting for transfers between devices: 123 us -> none  [the longest x1 123 us: local(): lax.all_to_all(mixed, 'tensor', split_axis=0, concat_axis=0, tiled=True)]
    convert_element_type x5 -> x0, local copies, waits for them, and re-layouts: 122 us -> none  [the longest x2 112 us: local(): query_prompt.astype(jnp.float32)]
    all_gather x1 -> x0, blocking collectives: 45.3 us -> none  [local(): lax.all_gather(output[prompt_own:], ('dp', 'tensor'), axis=0, tiled=True)]
    unnamed x114 -> x3, local copies, waits for them, and re-layouts: 47.6 us -> 4.54 us
    another operation x12 -> x0, other arithmetic: 28.2 us -> none
  transfers between devices with their start and end apart: 20 -> 0, of which waited for: 11 -> 0; matrix products, arithmetic and copies ran while one was open for 16% -> 0% of each run, Pallas kernels for 0% -> 0%
where the time goes in v1:
time: 138 us
  Pallas kernels  131 us (95%)
  local copies, waits for them, and re-layouts  5.86 us (4%)
    pallas_call x1, Pallas kernels, local(): pl.pallas_call(kernel, out_shape=(jax.ShapeDtypeStruct((2, 16, D), BF), j...  131 us
    unnamed x3, local copies, waits for them, and re-layouts  4.54 us

profile of v1, /device:TPU:1, one launch (start us, length us, event | category | flops | bytes accessed | tf_op | source)
XLA Modules:
  0.0 137.8 jit_solution(14624096603501500371)
XLA Ops:
  0.6 131.3 %decoder_layer.1 = (bf16[2,16,2048]{2,1,0:T(8,128)(2,1)}, bf16[1,2048]{1,0:T(2,128)(2,1)}, bf16[2,2,16,2048]{3,2,1,0:T(8,128)(2,1)}, bf16[2,1,2048]{2,1,0:T(2,128)(2,1)}) custom-call(bf16[2,16,2048]{2,1,0:T(8,128)(2,1)} %prompt_states.1, bf16[1,2048]{1,0:T(2,128)(2,1)} %decode_states.1, bf16[2,34,48,2048]{3,2,1,0:T(8,128)(2,1)} %cache.1, s32[8]{0:T(128)} %prompt_starts.1, ...), custom_call_target="tpu_custom_call" | custom-call | tf_op jit(solution)/shard_map/decoder_layer/pallas_call | solution.py:747
  131.9 1.3 copy.16
  133.2 1.6 %copy.20 = bf16[2,16,2048]{2,1,0:T(8,128)(2,1)} copy(bf16[2,16,2048]{2,1,0:T(8,128)(2,1)} %get-tuple-element.12) | data formatting | bytes 262144
  134.8 1.3 copy.21
  136.1 1.7 %copy.22 = bf16[2,2,16,2048]{3,2,1,0:T(8,128)(2,1)} copy(bf16[2,2,16,2048]{3,2,1,0:T(8,128)(2,1)} %get-tuple-element.14) | data formatting | bytes 524288

commit v2 on v1

v2 whole, which is shorter than its diff:
```python
import jax
import jax.numpy as jnp
import numpy as np
from jax import lax
from jax.experimental import pallas as pl
from jax.experimental.pallas import tpu as pltpu
from jax.sharding import PartitionSpec as P

D = 2048
HD = 128
HEADS = 16
FFD = 256
CTX = 48
EPSILON = 1e-06
ROPE_BASE = 500000.0
MASKED_SCORE = -1e30
LOG2E = 1.4426950408889634
SCALE = HD ** (-0.5)
BF = jnp.bfloat16
F32 = jnp.float32
MESH = pl.DeviceIdType.MESH
NT = (((1,), (1,)), ((), ()))


def mul(value, factor):
    return pl.multiple_of(value * factor, factor)


def remote(src, dst, send_sem, recv_sem, dev):
    return pltpu.make_async_remote_copy(
        src_ref=src,
        dst_ref=dst,
        send_sem=send_sem,
        recv_sem=recv_sem,
        device_id={"tensor": dev},
        device_id_type=MESH,
    )


class Plane:
    def __init__(self):
        self.y = lax.axis_index("dp")
        self.t = lax.axis_index("tensor")
        self.c = lax.rem(self.t, 2)
        self.q = lax.div(self.t, 2)
        x = lax.rem(self.q, 4)
        z = lax.div(self.q, 4)
        self.a = x + self.c * (z - x)
        self.b = z + self.c * (x - z)
        self.sib = self.t + 1 - 2 * self.c
        self.aR, self.aO, self.aL = [lax.rem(self.a + i, 4) for i in (1, 2, 3)]
        self.bR, self.bO, self.bL = [lax.rem(self.b + i, 4) for i in (1, 2, 3)]

    def chip(self, a, b):
        return a * (1 + 3 * self.c) + b * (4 - 3 * self.c)

    def dev(self, a, b):
        return 2 * self.chip(a, b) + self.c


def block(buf, chip):
    return buf.at[pl.ds(mul(chip, 32), 32)]


def half(buf, chip, h):
    return buf.at[pl.ds(mul(chip * 2 + h, 16), 16)]


def gather_steps(p, buf, ss, rs, sends):
    def send(slot, ref, dev):
        copy = remote(ref, ref, ss.at[slot], rs.at[slot], dev)
        copy.start()
        sends.append(copy)

    def recv(slot, ref):
        remote(ref, ref, ss.at[slot], rs.at[slot], p.dev(p.aR, p.b)).wait_recv()

    def blk(a, b):
        return block(buf, p.chip(a, b))

    def hlf(a, b, h):
        return half(buf, p.chip(a, b), h)

    a, b, aR, aL, aO, bR, bL, bO = p.a, p.b, p.aR, p.aL, p.aO, p.bR, p.bL, p.bO
    to_aR, to_aL, to_bR, to_bL = p.dev(aR, b), p.dev(aL, b), p.dev(a, bR), p.dev(a, bL)
    own = blk(a, b)
    send(0, own, to_aR)
    send(1, own, to_aL)
    send(4, own, to_bR)
    send(5, own, to_bL)
    yield
    recv(0, blk(aL, b))
    send(2, hlf(aL, b, 0), to_aR)
    send(8, blk(aL, b), to_bR)
    send(9, blk(aL, b), to_bL)
    recv(1, blk(aR, b))
    send(3, hlf(aR, b, 1), to_aL)
    send(12, blk(aR, b), to_bR)
    send(13, blk(aR, b), to_bL)
    yield
    recv(4, blk(a, bL))
    send(6, hlf(a, bL, 0), to_bR)
    recv(5, blk(a, bR))
    send(7, hlf(a, bR, 1), to_bL)
    yield
    recv(2, hlf(aO, b, 0))
    recv(3, hlf(aO, b, 1))
    send(16, blk(aO, b), to_bR)
    send(17, blk(aO, b), to_bL)
    yield
    columns = (a, aL, aR, aO)
    for k in (1, 2, 3):
        recv(4 + 4 * k, blk(columns[k], bL))
        send(6 + 4 * k, hlf(columns[k], bL, 0), to_bR)
        recv(5 + 4 * k, blk(columns[k], bR))
        send(7 + 4 * k, hlf(columns[k], bR, 1), to_bL)
        yield
        for done in (k - 1,) if k < 3 else (2, 3):
            recv(6 + 4 * done, hlf(columns[done], bO, 0))
            recv(7 + 4 * done, hlf(columns[done], bO, 1))
            yield columns[done]


def reduce_steps(p, buf, land, ss, rs, sends, out, make=None):
    def send(slot, ref, dev):
        copy = remote(ref, land.at[slot], ss.at[slot], rs.at[slot], dev)
        copy.start()
        sends.append(copy)

    def recv(slot):
        remote(land.at[slot], land.at[slot], ss.at[slot], rs.at[slot], p.dev(p.aR, p.b)).wait_recv()
        return land[slot].astype(F32)

    def hlf(a, b, h):
        return half(buf, p.chip(a, b), h)

    def add(ref, slots):
        total = ref[...].astype(F32)
        for slot in slots:
            total = total + recv(slot)
        return total

    a, b, aR, aL, aO, bR, bL, bO = p.a, p.b, p.aR, p.aL, p.aO, p.bR, p.bL, p.bO
    to_aR, to_aL, to_bR, to_bL = p.dev(aR, b), p.dev(aL, b), p.dev(a, bR), p.dev(a, bL)
    columns = {0: a, 1: aL, 2: aR, 3: aO}

    def first_hop(k):
        send(6 * k + 0, hlf(columns[k], bO, 0), to_bL)
        send(6 * k + 1, hlf(columns[k], bO, 1), to_bR)

    def second_hop(k):
        send(6 * k + 2, hlf(columns[k], bL, 1), to_bL)
        send(6 * k + 3, hlf(columns[k], bR, 0), to_bR)
        ref = hlf(columns[k], bL, 0)
        ref[...] = add(ref, (6 * k + 0,)).astype(BF)
        send(6 * k + 4, ref, to_bL)
        ref = hlf(columns[k], bR, 1)
        ref[...] = add(ref, (6 * k + 1,)).astype(BF)
        send(6 * k + 5, ref, to_bR)

    def column_sum(k):
        h0, h1 = hlf(columns[k], b, 0), hlf(columns[k], b, 1)
        h0[...] = add(h0, (6 * k + 3, 6 * k + 4)).astype(BF)
        h1[...] = add(h1, (6 * k + 2, 6 * k + 5)).astype(BF)
        return h0, h1

    for k in (3, 1, 2, 0):
        if make is not None:
            make(columns[k])
        first_hop(k)
    second_hop(3)
    yield
    second_hop(1)
    yield
    h0, h1 = column_sum(3)
    send(24, h0, to_aL)
    send(25, h1, to_aR)
    second_hop(2)
    yield
    h0, h1 = column_sum(1)
    send(26, h1, to_aL)
    second_hop(0)
    yield
    h0[...] = add(h0, (24,)).astype(BF)
    send(28, h0, to_aL)
    h0, h1 = column_sum(2)
    send(27, h0, to_aR)
    h1[...] = add(h1, (25,)).astype(BF)
    send(29, h1, to_aR)
    yield
    h0, h1 = column_sum(0)
    yield
    out.append(jnp.concatenate([add(h0, (27, 28)), add(h1, (26, 29))], axis=0))


def run(steps, tasks):
    tasks = list(tasks)
    for step in steps:
        if tasks:
            tasks.pop(0)()
    for task in tasks:
        task()


def turn(values, cosine, sine):
    lane = lax.broadcasted_iota(jnp.int32, values.shape, 1)
    swapped = jnp.where(lane % 2 == 0, pltpu.roll(values, HD - 1, 1), pltpu.roll(values, 1, 1))
    return values * cosine + swapped * sine


def angles(positions, freq):
    turned = positions * freq
    lane = lax.broadcasted_iota(jnp.int32, turned.shape, 1)
    return jnp.cos(turned), jnp.where(lane % 2 == 0, -1.0, 1.0) * jnp.sin(turned)


def kernel(
    prompt_states,
    decode_states,
    cache,
    prompt_starts,
    lengths,
    slots_row,
    slots,
    w_qkv,
    w_out,
    w_gate_up,
    w_down,
    gains,
    freq,
    prompt_out,
    decode_out,
    new_prompt_kv,
    new_decode_kv,
    X1,
    X2,
    Y,
    Y2,
    RB1,
    RB2,
    WQ,
    WO,
    WG,
    WD,
    KD,
    VD,
    CK,
    QR,
    KN,
    NKV,
    ACT,
    SS,
    DX,
    XD,
    DQ,
    DKV,
    QH,
    KH,
    LEN,
    DCS,
    OBF,
    OB,
    SB,
    OR,
    SR,
    DY,
    DR,
    DX2,
    DY2,
    DR2,
    PO,
    FIN,
    FS,
    FD,
    WIDE,
    WIDE3,
    TURNED,
    g1s,
    g1r,
    g2s,
    g2r,
    r1s,
    r1r,
    r2s,
    r2r,
    ws,
    wr,
    wl,
    ls,
    ms,
    mr,
    ys,
    yr,
):
    p = Plane()
    y, t, c, q, sib = p.y, p.t, p.c, p.q, p.sib
    sends = []
    lanes_q = pl.ds(mul(q, HD), HD)
    own_block = pl.ds(mul(q, 32), 32)

    barrier = pltpu.get_barrier_semaphore()

    @pl.loop(1, 32)
    def _(i):
        pl.semaphore_signal(
            barrier, inc=1, device_id={"tensor": lax.rem(t + i, 32)}, device_id_type=MESH
        )

    for i in (1, 2, 3):
        pl.semaphore_signal(barrier, inc=1, device_id={"dp": lax.rem(y + i, 4)}, device_id_type=MESH)

    def plane_peers(body):
        @pl.loop(1, 16)
        def _(i):
            chip = lax.rem(q + i, 16)
            body(chip, 2 * chip + c)

    def group_peers(body, first=1, last=32):
        @pl.loop(first, last)
        def _(i):
            body(lax.rem(t + i, 32))

    def drain_recv(ref, sem):
        remote(ref, ref, sem, sem, sib).wait_recv()

    def drain_send(ref, sem):
        remote(ref, ref, sem, sem, sib).wait_send()

    def local_copy(src, dst, sem):
        copy = pltpu.make_async_copy(src, dst, sem)
        copy.start()
        return copy

    piece_here = local_copy(prompt_states.at[c], half(X1, q, c), wl.at[0])
    weight_pairs = (
        (w_qkv, WQ.at[:, c]),
        (w_out, WO.at[c]),
        (w_gate_up, WG.at[c]),
        (w_down, WD.at[c]),
    )
    weights_here = [local_copy(src, dst, wl.at[1 + i]) for i, (src, dst) in enumerate(weight_pairs)]

    def cache_slice(dev):
        return cache.at[:, lax.rem(dev, 2), :, pl.ds(mul(lax.div(dev, 2), HD), HD)]

    loads = [
        local_copy(
            cache.at[kv, pl.ds(2 + 16 * part, 16)], dst.at[pl.ds(16 * part, 16)], ls.at[2 * kv + part]
        )
        for part in range(2)
        for kv, dst in ((0, KD), (1, VD))
    ]
    own_cache = local_copy(cache_slice(t), CK.at[:, t], wl.at[5])

    for j in range(HEADS):
        WIDE[pl.ds(j, 1), :] = decode_states[:, j * HD : (j + 1) * HD].astype(F32)
    DX[q] = WIDE[0:16, :].astype(BF)

    slot_row = lax.broadcasted_iota(jnp.int32, (32, HD), 0)
    slot_id = 32 * y + 2 * (slot_row % 16) + slot_row // 16
    matched = jnp.where(slots_row[...] == slot_id, lengths[...].astype(F32), 0.0)
    LEN[...] = jnp.broadcast_to(jnp.sum(matched, axis=1, keepdims=True), (32, HD))
    cosine, sine = angles(LEN[...], freq[...])
    DCS[0] = cosine
    DCS[1] = sine

    pl.semaphore_wait(barrier, 34)

    piece = remote(prompt_states.at[1 - c], half(X1, q, c), ws.at[0], wr.at[0], sib)
    piece.start()
    plane_peers(lambda chip, dev: remote(DX.at[q], DX.at[q], ms.at[0], mr.at[0], dev).start())
    weights_there = []
    for i, (src, dst) in enumerate(weight_pairs):
        weights_there.append(remote(src, dst, ws.at[1 + i], wr.at[1 + i], sib))
        weights_there[i].start()

    def weight_here(i):
        weights_here[i].wait()
        weights_there[i].wait_recv()

    piece_here.wait()
    piece.wait_recv()
    steps = gather_steps(p, X1, g1s, g1r, sends)
    next(steps)

    def rows_of(landed):
        WIDE3[...] = landed[...].astype(F32)
        return jnp.concatenate([WIDE3[:, j, :] for j in range(HEADS)], axis=1).astype(BF)

    def project(rows):
        return lax.dot_general(rows, WQ[...].reshape(3 * HD, D), NT, preferred_element_type=F32)

    drain_recv(DX.at[pl.ds(0, 15)], mr.at[0])
    XD[...] = rows_of(DX)
    weight_here(0)
    dec = project(XD[...]).astype(BF)
    DQ[c, :, lanes_q] = dec[:, :HD]
    DKV[0, :, lanes_q] = dec[:, HD : 2 * HD]
    DKV[1, :, lanes_q] = dec[:, 2 * HD :]
    q_own = DQ.at[c, :, lanes_q]
    kv_own = DKV.at[:, :, lanes_q]
    group_peers(lambda dev: remote(q_own, q_own, ms.at[2], mr.at[2], dev).start())
    plane_peers(lambda chip, dev: remote(kv_own, kv_own, ms.at[3], mr.at[3], dev).start())
    next(steps)

    def send_cache(first, last):
        group_peers(
            lambda dev: remote(cache_slice(dev), CK.at[:, t], ms.at[1], mr.at[1], dev).start(),
            first,
            last,
        )

    next(steps)
    next(steps)

    drain_recv(OR.at[pl.ds(0, 31)], mr.at[2])
    drain_recv(KN.at[:, pl.ds(0, 240)], mr.at[3])

    def normed(raw, gain_row, first):
        scale = lax.rsqrt(jnp.mean(raw * raw, axis=1, keepdims=True) + EPSILON)
        rows = raw.shape[0]
        cos_part, sin_part = DCS[0, pl.ds(first, rows), :], DCS[1, pl.ds(first, rows), :]
        parts = []
        for j in range(HEADS):
            lanes = slice(j * HD, (j + 1) * HD)
            scaled = raw[:, lanes] * scale * gains[gain_row : gain_row + 1, lanes]
            parts.append(turn(scaled, cos_part, sin_part).astype(BF).astype(F32))
        return parts

    for plane in range(2):
        for j, part in enumerate(normed(DQ[plane].astype(F32), 0, 16 * plane)):
            QH[16 * plane : 16 * plane + 16, j * HD : (j + 1) * HD] = part
    for j, part in enumerate(normed(DKV[0].astype(F32), 1, mul(c, 16))):
        KH[:, j * HD : (j + 1) * HD] = part
    for load in loads:
        load.wait()

    own_lane = lax.broadcasted_iota(jnp.int32, (HEADS, D), 1) // HD
    own_row = lax.broadcasted_iota(jnp.int32, (HEADS, D), 0)
    own_head = own_lane == own_row
    spot = (lax.broadcasted_iota(jnp.int32, (HEADS, CTX), 1) + CTX * t).astype(F32)
    stat_lane = lax.broadcasted_iota(jnp.int32, (HEADS, HD), 1)

    done = 0

    def decode_slots_at(r):
        for plane in range(2):
            tops, totals = [], []
            for upper in range(2):
                row = 8 * upper + r
                index = 16 * plane + row
                slot = 2 * row + plane
                spread = jnp.where(own_head, QH[pl.ds(index, 1), :], 0.0).astype(BF)
                scores = lax.dot_general(spread, KD[slot], NT, preferred_element_type=F32)
                live = spot < LEN[pl.ds(index, 1), :CTX]
                scores = jnp.where(live, scores * SCALE, MASKED_SCORE)
                top = jnp.max(scores, axis=1, keepdims=True)
                probs = jnp.where(live, jnp.exp(scores - top), 0.0)
                tops.append(top)
                totals.append(jnp.sum(probs, axis=1, keepdims=True))
                mixed = jnp.dot(probs.astype(BF), VD[slot], preferred_element_type=F32)
                OBF[pl.ds(index, 1), :] = jnp.sum(
                    jnp.where(own_head, mixed, 0.0), axis=0, keepdims=True
                )
            SB[plane, :, r, :] = jnp.where(
                stat_lane < 64,
                jnp.where(stat_lane < 32, tops[0], totals[0]),
                jnp.where(stat_lane < 96, tops[1], totals[1]),
            )

    stat_row = lax.broadcasted_iota(jnp.int32, (8, HD), 0)
    SS[q] = jnp.zeros((8, HD), F32)

    def column_blocks(a):
        return [pl.ds(mul(p.chip(a, i), 32), 32) for i in range(4)]

    def row_sums(values):
        total = jnp.sum(values * values, axis=1, keepdims=True)
        return jnp.broadcast_to(total, (HD, HD)).T[0:8, :]

    def column_project(a):
        rows = pl.ds(mul(a, HD), HD)
        got = project(jnp.concatenate([X1[place, :] for place in column_blocks(a)], axis=0)).astype(BF)
        QR[rows, :] = got[:, :HD]
        KN[0, rows, :] = got[:, HD : 2 * HD]
        KN[1, rows, :] = got[:, 2 * HD :]
        query_sum = row_sums(got[:, :HD].astype(F32))
        key_sum = row_sums(got[:, HD : 2 * HD].astype(F32))
        SS[q] = jnp.where(
            stat_row == a, query_sum, jnp.where(stat_row == 4 + a, key_sum, SS[q])
        )

    turn_no = 0
    for step in steps:
        if step is None:
            if turn_no == 2:
                send_cache(1, 16)
            turn_no += 1
        else:
            column_project(step)
        if done < 8:
            decode_slots_at(done)
            done += 1
    plane_peers(lambda chip, dev: remote(SS.at[q], SS.at[q], ms.at[6], mr.at[6], dev).start())
    send_cache(16, 32)
    for r in range(done, 8):
        decode_slots_at(r)

    OB[0] = OBF[0:16, :].astype(BF)
    OB[1] = OBF[16:32, :].astype(BF)

    def mixed_slice(dev):
        return OB.at[lax.rem(dev, 2), :, pl.ds(mul(lax.div(dev, 2), HD), HD)]

    def stat_slice(dev):
        return SB.at[lax.rem(dev, 2), lax.div(dev, 2)]

    own_mixed = local_copy(mixed_slice(t), OR.at[t], wl.at[6])
    own_stat = local_copy(stat_slice(t), SR.at[t], wl.at[7])

    def send_partial(dev):
        remote(mixed_slice(dev), OR.at[t], ms.at[4], mr.at[4], dev).start()
        remote(stat_slice(dev), SR.at[t], ms.at[5], mr.at[5], dev).start()

    group_peers(send_partial)

    start = prompt_starts[2 * y + c]

    def offsets_of(index):
        chips = (index // HD) * (1 + 3 * c) + (index // 32 % 4) * (4 - 3 * c)
        return chips * 32 + index % 32

    for i in range(4):
        rows = slice(i * HD, (i + 1) * HD)
        offset = offsets_of(lax.broadcasted_iota(jnp.int32, (HD, HD), 0) + i * HD)
        cosine, sine = angles((offset + start).astype(F32), freq[...])
        for kind in range(2):
            raw = (QR[rows, :] if kind == 0 else KN[0, rows, :]).astype(F32)
            TURNED[kind, rows, :] = turn(raw * gains[kind : kind + 1, lanes_q], cosine, sine)
    drain_recv(SS.at[pl.ds(0, 15)], mr.at[6])
    scales = lax.rsqrt(jnp.sum(SS[...], axis=0) * (1.0 / D) + EPSILON)
    for i in range(4):
        rows = slice(i * HD, (i + 1) * HD)
        for kind in range(2):
            column = jnp.broadcast_to(scales[4 * kind + i : 4 * kind + i + 1, :], (HD, HD)).T
            turned = (TURNED[kind, rows, :] * column).astype(BF)
            if kind == 0:
                QR[rows, :] = turned
            else:
                KN[0, rows, :] = turned

    def fresh_slice(dev):
        chip = lax.div(dev, 2)
        low, high = lax.rem(chip, 4), lax.div(chip, 4)
        a, b = low + c * (high - low), high + c * (low - high)
        return KN.at[:, pl.ds(mul(8 * a + 2 * b + lax.rem(dev, 2), 16), 16), :]

    landing = NKV.at[:, c, :, lanes_q]
    own_fresh = local_copy(fresh_slice(t), landing, wl.at[8])
    group_peers(lambda dev: remote(fresh_slice(dev), landing, ms.at[7], mr.at[7], dev).start())

    own_mixed.wait()
    own_stat.wait()
    drain_recv(OR.at[pl.ds(0, 31)], mr.at[4])
    drain_recv(SR.at[pl.ds(0, 31)], mr.at[5])

    def stat(lane):
        parts = [
            jnp.broadcast_to(SR[:, :, lane + 64 * k : lane + 64 * k + 1], (32, 8, HD)) for k in (0, 1)
        ]
        return jnp.concatenate(parts, axis=1)

    tops, totals = stat(0), stat(32)
    own_rows = pl.ds(mul(c, 16), 16)
    own_score = (
        jnp.sum(QH[own_rows, lanes_q] * KH[:, lanes_q], axis=1, keepdims=True) * SCALE
    )
    highest = jnp.maximum(jnp.max(tops, axis=0), own_score)
    factors = jnp.exp(tops - highest[None])
    own_weight = jnp.exp(own_score - highest)
    total = jnp.sum(totals * factors, axis=0) + own_weight
    mixed = jnp.sum(OR[...].astype(F32) * factors, axis=0)
    mixed = mixed + own_weight.astype(BF).astype(F32) * DKV[1, :, lanes_q].astype(F32)
    attended_rows = (mixed / total).astype(BF)

    weight_here(1)

    def spread_decode(tail, staged, landed, index):
        for j in range(HEADS):
            WIDE3[:, j, :] = tail[:, j * HD : (j + 1) * HD]
        staged[...] = WIDE3[...].astype(BF)
        landed[q] = staged[q]
        plane_peers(
            lambda chip, dev: remote(
                staged.at[chip], landed.at[q], ms.at[index], mr.at[index], dev
            ).start()
        )

    def row_of(gain):
        parts = [gains[gain : gain + 1, j * HD : (j + 1) * HD] for j in range(HEADS)]
        return jnp.concatenate(parts, axis=0)

    def add_normed_rows(base, total, gain):
        scale = lax.rsqrt(jnp.mean(total * total, axis=1, keepdims=True) + EPSILON)
        return (base + total * scale * gains[gain : gain + 1, :]).astype(BF)

    def add_normed_row(base, landed, gain):
        total = jnp.sum(landed[...].astype(F32), axis=0)
        square = jnp.sum(total * total, axis=1, keepdims=True)
        mean = jnp.sum(square, axis=0, keepdims=True) * (1.0 / D)
        scale = lax.rsqrt(mean + EPSILON)
        return (base.astype(F32) + total * scale * row_of(gain)).astype(BF)

    w_head = WO[...].reshape(HD, D)
    spread_decode(jnp.dot(attended_rows, w_head, preferred_element_type=F32), DY, DR, 8)

    own_cache.wait()
    drain_recv(CK.at[:, pl.ds(0, 31)], mr.at[1])
    cached_spot = lax.broadcasted_iota(jnp.int32, (1, 32 * CTX), 1)
    cached_bias = jnp.where(cached_spot < start, 0.0, MASKED_SCORE)

    def column_attend(a):
        query = QR[pl.ds(mul(a, HD), HD), :]
        cached_keys = CK[0].reshape(32 * CTX, HD)
        cached_values = CK[1].reshape(32 * CTX, HD)
        fresh = lax.dot_general(query, KN[0], NT, preferred_element_type=F32)
        cached = lax.dot_general(query, cached_keys, NT, preferred_element_type=F32)
        column = offsets_of(lax.broadcasted_iota(jnp.int32, (1, 512), 1))
        row = offsets_of(lax.broadcasted_iota(jnp.int32, (HD, 1), 0) + a * HD)
        fresh = jnp.where(column <= row, fresh, MASKED_SCORE)
        cached = cached + cached_bias
        top = jnp.maximum(
            jnp.max(fresh, axis=1, keepdims=True), jnp.max(cached, axis=1, keepdims=True)
        )
        fresh = jnp.exp2((fresh - top) * (SCALE * LOG2E))
        cached = jnp.exp2((cached - top) * (SCALE * LOG2E))
        total = jnp.sum(fresh, axis=1, keepdims=True) + jnp.sum(cached, axis=1, keepdims=True)
        mixed = jnp.dot(fresh.astype(BF), KN[1], preferred_element_type=F32)
        mixed = mixed + jnp.dot(cached.astype(BF), cached_values, preferred_element_type=F32)
        result = jnp.dot(
            (mixed / total).astype(BF), w_head, preferred_element_type=F32
        ).astype(BF)
        for i, place in enumerate(column_blocks(a)):
            Y[place, :] = result[32 * i : 32 * i + 32]

    def hidden_row():
        drain_recv(DR.at[pl.ds(0, 15)], mr.at[8])
        DX2[q] = add_normed_row(DX[q], DR, 2)
        plane_peers(lambda chip, dev: remote(DX2.at[q], DX2.at[q], ms.at[9], mr.at[9], dev).start())

    attn_rows = []
    nothing = lambda: None
    run(
        reduce_steps(p, Y, RB1, r1s, r1r, sends, attn_rows, column_attend),
        [nothing, nothing, hidden_row],
    )
    X2[own_block, :] = add_normed_rows(X1[own_block, :].astype(F32), attn_rows[0], 2)
    steps = gather_steps(p, X2, g2s, g2r, sends)
    next(steps)

    weight_here(2)
    weight_here(3)

    def gated(hidden, core):
        gate = jnp.dot(hidden, WG[core, 0], preferred_element_type=F32)
        up = jnp.dot(hidden, WG[core, 1], preferred_element_type=F32)
        return (gate / (1.0 + jnp.exp(-gate)) * up).astype(BF)

    def down(pair):
        return jnp.dot(pair[0], WD[0], preferred_element_type=F32) + jnp.dot(
            pair[1], WD[1], preferred_element_type=F32
        )

    def decode_ffn():
        drain_recv(DX2.at[pl.ds(0, 15)], mr.at[9])
        hidden = rows_of(DX2)
        spread_decode(down([gated(hidden, core) for core in range(2)]), DY2, DR2, 10)

    def final_row():
        drain_recv(DR2.at[pl.ds(0, 15)], mr.at[10])
        FIN[t] = add_normed_row(DX2[q], DR2, 3)
        group_peers(lambda dev: remote(FIN.at[t], FIN.at[t], ms.at[11], mr.at[11], dev).start())

    def column_gated(a):
        hidden = jnp.concatenate([X2[rows, :] for rows in column_blocks(a)], axis=0)
        for core in range(2):
            ACT[core, pl.ds(mul(a, HD), HD), :] = gated(hidden, core)

    def column_down(a):
        rows = pl.ds(mul(a, HD), HD)
        result = down([ACT[0, rows, :], ACT[1, rows, :]]).astype(BF)
        for i, place in enumerate(column_blocks(a)):
            Y2[place, :] = result[32 * i : 32 * i + 32]

    mine = lax.broadcasted_iota(jnp.int32, (16, D), 0) == q

    def own_row_of(rows):
        return jnp.sum(jnp.where(mine, rows, 0.0), axis=0, keepdims=True).astype(BF)

    def fresh_out():
        own_fresh.wait()
        drain_recv(KN.at[:, pl.ds(0, 496)], mr.at[7])
        new_prompt_kv[...] = NKV[...]
        new_decode_kv[0, 0:1, :] = own_row_of(KH[...])
        new_decode_kv[0, 1:2, :] = own_row_of(DKV[1].astype(F32))

    tasks = [nothing, decode_ffn, fresh_out, final_row]
    for step in steps:
        if step is not None:
            column_gated(step)
        elif tasks:
            tasks.pop(0)()
    for task in tasks:
        task()

    slot_of = lax.broadcasted_iota(jnp.int32, (32, 16, HD), 0) + 32 * y
    crossing = []

    def wanted_row(yy):
        wanted = slots[32 * yy + t]
        return jnp.sum(jnp.where(slot_of == wanted, FIN[...].astype(F32), 0.0), axis=0)

    def cross_rows():
        drain_recv(FIN.at[pl.ds(0, 31)], mr.at[11])
        FD[0] = wanted_row(y)
        for i in (1, 2, 3):
            other = lax.rem(y + i, 4)
            FD[3 + i] = wanted_row(other)
            copy = pltpu.make_async_remote_copy(
                src_ref=FD.at[3 + i],
                dst_ref=FD.at[i],
                send_sem=ys.at[i - 1],
                recv_sem=yr.at[i - 1],
                device_id={"dp": other},
                device_id_type=MESH,
            )
            copy.start()
            crossing.append(copy)

    def decode_rows_out():
        result = FD[0]
        for i, copy in enumerate(crossing):
            copy.wait_recv()
            result = result + FD[1 + i]
        for j in range(HEADS):
            decode_out[:, j * HD : (j + 1) * HD] = result[j : j + 1, :].astype(BF)

    ffn_rows = []
    run(
        reduce_steps(p, Y2, RB2, r2s, r2r, sends, ffn_rows, column_down),
        [cross_rows, nothing, nothing, decode_rows_out],
    )
    out_rows = add_normed_rows(X2[own_block, :].astype(F32), ffn_rows[0], 3)
    FS[...] = out_rows.reshape(2, 16, D)
    swap = remote(FS.at[1 - c], PO.at[c], ws.at[5], wr.at[5], sib)
    swap.start()
    PO[c] = FS[c]

    for copy in sends + crossing + [piece]:
        copy.wait_send()
    for there in weights_there:
        there.wait_send()
    drain_send(DX.at[pl.ds(0, 15)], ms.at[0])
    drain_send(CK.at[:, pl.ds(0, 31)], ms.at[1])
    drain_send(OR.at[pl.ds(0, 31)], ms.at[2])
    drain_send(KN.at[:, pl.ds(0, 240)], ms.at[3])
    drain_send(OR.at[pl.ds(0, 31)], ms.at[4])
    drain_send(SR.at[pl.ds(0, 31)], ms.at[5])
    drain_send(SS.at[pl.ds(0, 15)], ms.at[6])
    drain_send(KN.at[:, pl.ds(0, 496)], ms.at[7])
    drain_send(DR.at[pl.ds(0, 15)], ms.at[8])
    drain_send(DX2.at[pl.ds(0, 15)], ms.at[9])
    drain_send(DR2.at[pl.ds(0, 15)], ms.at[10])
    drain_send(FIN.at[pl.ds(0, 31)], ms.at[11])
    swap.wait()
    prompt_out[...] = PO[...]


def place(*refs):
    for src, dst in zip(refs[:4], refs[4:]):
        dst[...] = src[...]


def local(
    prompt_states,
    decode_states,
    cache,
    prompt_starts,
    decode_lengths,
    decode_slots,
    w_qkv,
    w_out,
    w_gate_up,
    w_down,
    gains,
):
    freq = np.power(ROPE_BASE, -2.0 * (np.arange(HD) // 2) / HD).astype(np.float32)[None, :]
    vmem = pl.BlockSpec(memory_space=pltpu.VMEM)
    smem = pl.BlockSpec(memory_space=pltpu.SMEM)
    hbm = pl.BlockSpec(memory_space=pl.ANY)
    scratch = [
        ((512, D), BF),
        ((512, D), BF),
        ((512, D), BF),
        ((512, D), BF),
        ((30, 16, D), BF),
        ((30, 16, D), BF),
        ((3, 2, 64, D), BF),
        ((2, 64, D), BF),
        ((2, 2, D, FFD), BF),
        ((2, FFD, D), BF),
        ((32, CTX, D), BF),
        ((32, CTX, D), BF),
        ((2, 32, CTX, HD), BF),
        ((512, HD), BF),
        ((2, 512, HD), BF),
        ((2, 2, 16, D), BF),
        ((2, 512, FFD), BF),
        ((16, 8, HD), F32),
        ((16, 16, HD), BF),
        ((16, D), BF),
        ((2, 16, D), BF),
        ((2, 16, D), BF),
        ((32, D), F32),
        ((16, D), F32),
        ((32, HD), F32),
        ((2, 32, HD), F32),
        ((32, D), F32),
        ((2, 16, D), BF),
        ((2, 16, 8, HD), F32),
        ((32, 16, HD), BF),
        ((32, 8, HD), F32),
        ((16, 16, HD), BF),
        ((16, 16, HD), BF),
        ((16, 16, HD), BF),
        ((16, 16, HD), BF),
        ((16, 16, HD), BF),
        ((2, 16, D), BF),
        ((32, 16, HD), BF),
        ((2, 16, D), BF),
        ((7, 16, HD), F32),
        ((16, HD), F32),
        ((16, 16, HD), F32),
        ((2, 512, HD), F32),
    ]
    sems = [20, 20, 20, 20, 30, 30, 30, 30, 6, 6, 9, 4, 12, 12, 3, 3]
    outs = pl.pallas_call(
        kernel,
        out_shape=(
            jax.ShapeDtypeStruct((2, 16, D), BF),
            jax.ShapeDtypeStruct((1, D), BF),
            jax.ShapeDtypeStruct((2, 2, 16, D), BF),
            jax.ShapeDtypeStruct((1, 2, D), BF),
        ),
        in_specs=[hbm, vmem, hbm, smem, vmem, vmem, smem, hbm, hbm, hbm, hbm, vmem, vmem],
        out_specs=(vmem, vmem, vmem, vmem),
        scratch_shapes=[pltpu.VMEM(shape, dtype) for shape, dtype in scratch]
        + [pltpu.SemaphoreType.DMA((count,)) for count in sems],
        compiler_params=pltpu.CompilerParams(
            collective_id=0, has_side_effects=True, vmem_limit_bytes=60 * 1024 * 1024
        ),
        name="decoder_layer",
    )(
        prompt_states,
        decode_states,
        cache,
        prompt_starts,
        decode_lengths[None, :],
        decode_slots[None, :],
        decode_slots,
        jnp.swapaxes(w_qkv, 1, 2),
        w_out,
        w_gate_up,
        w_down,
        gains,
        jnp.asarray(freq),
    )
    placed = pl.pallas_call(
        place,
        out_shape=tuple(jax.ShapeDtypeStruct(out.shape, out.dtype) for out in outs),
        in_specs=[vmem] * 4,
        out_specs=(vmem,) * 4,
        name="place",
    )(*outs)
    return placed[0], placed[1], placed[2], jnp.swapaxes(placed[3], 0, 1)


def solution(mesh):
    in_specs = (
        P("dp", "tensor", None),
        P(("dp", "tensor"), None),
        P(None, "dp", "tensor", None),
        P(),
        P(),
        P(),
        P(None, None, "tensor"),
        P("tensor", None),
        P(None, None, "tensor"),
        P("tensor", None),
        P(),
    )
    out_specs = (
        P("dp", "tensor", None),
        P(("dp", "tensor"), None),
        P(None, "dp", "tensor", None),
        P(None, ("dp", "tensor"), None),
    )
    return jax.shard_map(local, mesh=mesh, in_specs=in_specs, out_specs=out_specs, check_vma=False)
```

time: 138 us -> 117 us (0.85)
  Pallas kernels: 131 us -> 116 us
  local copies, waits for them, and re-layouts: 5.86 us -> 0 us
    pallas_call x1, Pallas kernels: 131 us -> 114 us  [local(): pl.pallas_call(kernel, out_shape=(jax.ShapeDtypeStruct((2, 16, D), BF), j...]
    unnamed x3 -> x0, local copies, waits for them, and re-layouts: 4.54 us -> none
    pallas_call x0 -> x1, Pallas kernels: none -> 1.8 us  [local(): pl.pallas_call(place, out_shape=tuple((jax.ShapeDtypeStruct(out.shape, ou...]
where the time goes in v2:
time: 117 us
  Pallas kernels  116 us (99%)
    pallas_call x1, Pallas kernels, local(): pl.pallas_call(kernel, out_shape=(jax.ShapeDtypeStruct((2, 16, D), BF), j...  114 us

profile of v2, /device:TPU:1, one launch (start us, length us, event | category | flops | bytes accessed | tf_op | source)
XLA Modules:
  0.0 116.8 jit_solution(1747818940423162655)
XLA Ops:
  0.6 114.4 %decoder_layer.1 = (bf16[2,16,2048]{2,1,0:T(8,128)(2,1)}, bf16[1,2048]{1,0:T(2,128)(2,1)}, bf16[2,2,16,2048]{3,2,1,0:T(8,128)(2,1)}, bf16[1,2,2048]{2,1,0:T(2,128)(2,1)}) custom-call(bf16[2,16,2048]{2,1,0:T(8,128)(2,1)} %prompt_states.1, bf16[1,2048]{1,0:T(2,128)(2,1)} %decode_states.1, bf16[2,34,48,2048]{3,2,1,0:T(8,128)(2,1)} %cache.1, s32[8]{0:T(128)} %prompt_starts.1, ...), custom_call_target="tpu_custom_call" | custom-call | tf_op jit(solution)/shard_map/decoder_layer/pallas_call | solution.py:847
  115.0 1.8 %place.1 = (bf16[2,16,2048]{2,1,0:T(8,128)(2,1)}, bf16[1,2048]{1,0:T(2,128)(2,1)}, bf16[2,2,16,2048]{3,2,1,0:T(8,128)(2,1)}, bf16[1,2,2048]{2,1,0:T(2,128)(2,1)}) custom-call(bf16[2,16,2048]{2,1,0:T(8,128)(2,1)} %get-tuple-element.12.refs_0_, bf16[1,2048]{1,0:T(2,128)(2,1)} %get-tuple-element.13.refs_1_, bf16[2,2,16,2048]{3,2,1,0:T(8,128)(2,1)} %get-tuple-element.14.refs_2_, ...), custom_call_target="tpu_custom_call" | custom-call | tf_op jit(solution)/shard_map/place/pallas_call | solution.py:878

commit v3 on v2

--- a/solution.py
+++ b/solution.py
@@ -86,15 +86,14 @@
     own = blk(a, b)
     send(0, own, to_aR)
     send(1, own, to_aL)
+    send(2, own, p.dev(aO, b))
     send(4, own, to_bR)
     send(5, own, to_bL)
     yield
     recv(0, blk(aL, b))
-    send(2, hlf(aL, b, 0), to_aR)
     send(8, blk(aL, b), to_bR)
     send(9, blk(aL, b), to_bL)
     recv(1, blk(aR, b))
-    send(3, hlf(aR, b, 1), to_aL)
     send(12, blk(aR, b), to_bR)
     send(13, blk(aR, b), to_bL)
     yield
@@ -103,8 +102,7 @@
     recv(5, blk(a, bR))
     send(7, hlf(a, bR, 1), to_bL)
     yield
-    recv(2, hlf(aO, b, 0))
-    recv(3, hlf(aO, b, 1))
+    recv(2, blk(aO, b))
     send(16, blk(aO, b), to_bR)
     send(17, blk(aO, b), to_bL)
     yield
@@ -115,91 +113,63 @@
         recv(5 + 4 * k, blk(columns[k], bR))
         send(7 + 4 * k, hlf(columns[k], bR, 1), to_bL)
         yield
-        for done in (k - 1,) if k < 3 else (2, 3):
+        for done in ((), (), (0,), (1, 2, 3))[k]:
             recv(6 + 4 * done, hlf(columns[done], bO, 0))
             recv(7 + 4 * done, hlf(columns[done], bO, 1))
             yield columns[done]
 
 
-def reduce_steps(p, buf, land, ss, rs, sends, out, make=None):
-    def send(slot, ref, dev):
-        copy = remote(ref, land.at[slot], ss.at[slot], rs.at[slot], dev)
+class Reduce:
+    def __init__(self, p, buf, land, ss, rs, sends):
+        self.p, self.buf, self.land, self.ss, self.rs, self.sends = p, buf, land, ss, rs, sends
+        self.columns = (p.a, p.aL, p.aR, p.aO)
+        self.owners = [p.dev(column, p.b) for column in self.columns]
+        self.to_bR, self.to_bL = p.dev(p.a, p.bR), p.dev(p.a, p.bL)
+
+    def place(self, slot):
+        return self.land.at[pl.ds(16 * slot, 16 if slot < 24 else 32)]
+
+    def send(self, slot, ref, dev):
+        copy = remote(ref, self.place(slot), self.ss.at[slot], self.rs.at[slot], dev)
         copy.start()
-        sends.append(copy)
-
-    def recv(slot):
-        remote(land.at[slot], land.at[slot], ss.at[slot], rs.at[slot], p.dev(p.aR, p.b)).wait_recv()
-        return land[slot].astype(F32)
-
-    def hlf(a, b, h):
-        return half(buf, p.chip(a, b), h)
-
-    def add(ref, slots):
+        self.sends.append(copy)
+
+    def add(self, ref, slots):
         total = ref[...].astype(F32)
         for slot in slots:
-            total = total + recv(slot)
+            place = self.place(slot)
+            remote(place, place, self.ss.at[slot], self.rs.at[slot], self.to_bR).wait_recv()
+            total = total + place[...].astype(F32)
         return total
 
-    a, b, aR, aL, aO, bR, bL, bO = p.a, p.b, p.aR, p.aL, p.aO, p.bR, p.bL, p.bO
-    to_aR, to_aL, to_bR, to_bL = p.dev(aR, b), p.dev(aL, b), p.dev(a, bR), p.dev(a, bL)
-    columns = {0: a, 1: aL, 2: aR, 3: aO}
-
-    def first_hop(k):
-        send(6 * k + 0, hlf(columns[k], bO, 0), to_bL)
-        send(6 * k + 1, hlf(columns[k], bO, 1), to_bR)
-
-    def second_hop(k):
-        send(6 * k + 2, hlf(columns[k], bL, 1), to_bL)
-        send(6 * k + 3, hlf(columns[k], bR, 0), to_bR)
-        ref = hlf(columns[k], bL, 0)
-        ref[...] = add(ref, (6 * k + 0,)).astype(BF)
-        send(6 * k + 4, ref, to_bL)
-        ref = hlf(columns[k], bR, 1)
-        ref[...] = add(ref, (6 * k + 1,)).astype(BF)
-        send(6 * k + 5, ref, to_bR)
-
-    def column_sum(k):
-        h0, h1 = hlf(columns[k], b, 0), hlf(columns[k], b, 1)
-        h0[...] = add(h0, (6 * k + 3, 6 * k + 4)).astype(BF)
-        h1[...] = add(h1, (6 * k + 2, 6 * k + 5)).astype(BF)
-        return h0, h1
-
-    for k in (3, 1, 2, 0):
-        if make is not None:
-            make(columns[k])
-        first_hop(k)
-    second_hop(3)
-    yield
-    second_hop(1)
-    yield
-    h0, h1 = column_sum(3)
-    send(24, h0, to_aL)
-    send(25, h1, to_aR)
-    second_hop(2)
-    yield
-    h0, h1 = column_sum(1)
-    send(26, h1, to_aL)
-    second_hop(0)
-    yield
-    h0[...] = add(h0, (24,)).astype(BF)
-    send(28, h0, to_aL)
-    h0, h1 = column_sum(2)
-    send(27, h0, to_aR)
-    h1[...] = add(h1, (25,)).astype(BF)
-    send(29, h1, to_aR)
-    yield
-    h0, h1 = column_sum(0)
-    yield
-    out.append(jnp.concatenate([add(h0, (27, 28)), add(h1, (26, 29))], axis=0))
-
-
-def run(steps, tasks):
-    tasks = list(tasks)
-    for step in steps:
-        if tasks:
-            tasks.pop(0)()
-    for task in tasks:
-        task()
+    def half(self, k, b, h):
+        return half(self.buf, self.p.chip(self.columns[k], b), h)
+
+    def first_hop(self, k):
+        self.send(6 * k + 0, self.half(k, self.p.bO, 0), self.to_bL)
+        self.send(6 * k + 1, self.half(k, self.p.bO, 1), self.to_bR)
+
+    def leaves(self, k):
+        self.send(6 * k + 2, self.half(k, self.p.bL, 1), self.to_bL)
+        self.send(6 * k + 3, self.half(k, self.p.bR, 0), self.to_bR)
+
+    def second_hop(self, k):
+        ref = self.half(k, self.p.bL, 0)
+        ref[...] = self.add(ref, (6 * k + 0,)).astype(BF)
+        self.send(6 * k + 4, ref, self.to_bL)
+        ref = self.half(k, self.p.bR, 1)
+        ref[...] = self.add(ref, (6 * k + 1,)).astype(BF)
+        self.send(6 * k + 5, ref, self.to_bR)
+
+    def column_sum(self, k):
+        h0, h1 = self.half(k, self.p.b, 0), self.half(k, self.p.b, 1)
+        h0[...] = self.add(h0, (6 * k + 3, 6 * k + 4)).astype(BF)
+        h1[...] = self.add(h1, (6 * k + 2, 6 * k + 5)).astype(BF)
+        if k > 0:
+            self.send(22 + 2 * k, block(self.buf, self.p.chip(self.columns[k], self.p.b)), self.owners[k])
+
+    def own_sum(self):
+        return self.add(block(self.buf, self.p.chip(self.p.a, self.p.b)), (24, 26, 28))
 
 
 def turn(values, cosine, sine):
@@ -343,6 +313,29 @@
     def cache_slice(dev):
         return cache.at[:, lax.rem(dev, 2), :, pl.ds(mul(lax.div(dev, 2), HD), HD)]
 
+    own_cache = local_copy(cache_slice(t), CK.at[:, t], wl.at[5])
+
+    for j in range(HEADS):
+        WIDE[pl.ds(j, 1), :] = decode_states[:, j * HD : (j + 1) * HD].astype(F32)
+    DX[q] = WIDE[0:16, :].astype(BF)
+
+    slot_row = lax.broadcasted_iota(jnp.int32, (32, HD), 0)
+    slot_id = 32 * y + 2 * (slot_row % 16) + slot_row // 16
+    matched = jnp.where(slots_row[...] == slot_id, lengths[...].astype(F32), 0.0)
+    LEN[...] = jnp.broadcast_to(jnp.sum(matched, axis=1, keepdims=True), (32, HD))
+    cosine, sine = angles(LEN[...], freq[...])
+    DCS[0] = cosine
+    DCS[1] = sine
+
+    pl.semaphore_wait(barrier, 34)
+
+    piece = remote(prompt_states.at[1 - c], half(X1, q, c), ws.at[0], wr.at[0], sib)
+    piece.start()
+    plane_peers(lambda chip, dev: remote(DX.at[q], DX.at[q], ms.at[0], mr.at[0], dev).start())
+    weights_there = []
+    for i, (src, dst) in enumerate(weight_pairs):
+        weights_there.append(remote(src, dst, ws.at[1 + i], wr.at[1 + i], sib))
+    weights_there[0].start()
     loads = [
         local_copy(
             cache.at[kv, pl.ds(2 + 16 * part, 16)], dst.at[pl.ds(16 * part, 16)], ls.at[2 * kv + part]
@@ -350,34 +343,21 @@
         for part in range(2)
         for kv, dst in ((0, KD), (1, VD))
     ]
-    own_cache = local_copy(cache_slice(t), CK.at[:, t], wl.at[5])
-
-    for j in range(HEADS):
-        WIDE[pl.ds(j, 1), :] = decode_states[:, j * HD : (j + 1) * HD].astype(F32)
-    DX[q] = WIDE[0:16, :].astype(BF)
-
-    slot_row = lax.broadcasted_iota(jnp.int32, (32, HD), 0)
-    slot_id = 32 * y + 2 * (slot_row % 16) + slot_row // 16
-    matched = jnp.where(slots_row[...] == slot_id, lengths[...].astype(F32), 0.0)
-    LEN[...] = jnp.broadcast_to(jnp.sum(matched, axis=1, keepdims=True), (32, HD))
-    cosine, sine = angles(LEN[...], freq[...])
-    DCS[0] = cosine
-    DCS[1] = sine
-
-    pl.semaphore_wait(barrier, 34)
-
-    piece = remote(prompt_states.at[1 - c], half(X1, q, c), ws.at[0], wr.at[0], sib)
-    piece.start()
-    plane_peers(lambda chip, dev: remote(DX.at[q], DX.at[q], ms.at[0], mr.at[0], dev).start())
-    weights_there = []
-    for i, (src, dst) in enumerate(weight_pairs):
-        weights_there.append(remote(src, dst, ws.at[1 + i], wr.at[1 + i], sib))
+    for i in (1, 2, 3):
         weights_there[i].start()
 
     def weight_here(i):
         weights_here[i].wait()
         weights_there[i].wait_recv()
 
+    def send_cache(first, last):
+        group_peers(
+            lambda dev: remote(cache_slice(dev), CK.at[:, t], ms.at[1], mr.at[1], dev).start(),
+            first,
+            last,
+        )
+
+    send_cache(1, 8)
     piece_here.wait()
     piece.wait_recv()
     steps = gather_steps(p, X1, g1s, g1r, sends)
@@ -390,6 +370,8 @@
     def project(rows):
         return lax.dot_general(rows, WQ[...].reshape(3 * HD, D), NT, preferred_element_type=F32)
 
+    next(steps)
+    next(steps)
     drain_recv(DX.at[pl.ds(0, 15)], mr.at[0])
     XD[...] = rows_of(DX)
     weight_here(0)
@@ -403,19 +385,6 @@
     plane_peers(lambda chip, dev: remote(kv_own, kv_own, ms.at[3], mr.at[3], dev).start())
     next(steps)
 
-    def send_cache(first, last):
-        group_peers(
-            lambda dev: remote(cache_slice(dev), CK.at[:, t], ms.at[1], mr.at[1], dev).start(),
-            first,
-            last,
-        )
-
-    next(steps)
-    next(steps)
-
-    drain_recv(OR.at[pl.ds(0, 31)], mr.at[2])
-    drain_recv(KN.at[:, pl.ds(0, 240)], mr.at[3])
-
     def normed(raw, gain_row, first):
         scale = lax.rsqrt(jnp.mean(raw * raw, axis=1, keepdims=True) + EPSILON)
         rows = raw.shape[0]
@@ -427,21 +396,22 @@
             parts.append(turn(scaled, cos_part, sin_part).astype(BF).astype(F32))
         return parts
 
-    for plane in range(2):
-        for j, part in enumerate(normed(DQ[plane].astype(F32), 0, 16 * plane)):
-            QH[16 * plane : 16 * plane + 16, j * HD : (j + 1) * HD] = part
-    for j, part in enumerate(normed(DKV[0].astype(F32), 1, mul(c, 16))):
-        KH[:, j * HD : (j + 1) * HD] = part
-    for load in loads:
-        load.wait()
+    def decode_norms():
+        drain_recv(OR.at[pl.ds(0, 31)], mr.at[2])
+        drain_recv(KN.at[:, pl.ds(0, 240)], mr.at[3])
+        for plane in range(2):
+            for j, part in enumerate(normed(DQ[plane].astype(F32), 0, 16 * plane)):
+                QH[16 * plane : 16 * plane + 16, j * HD : (j + 1) * HD] = part
+        for j, part in enumerate(normed(DKV[0].astype(F32), 1, mul(c, 16))):
+            KH[:, j * HD : (j + 1) * HD] = part
+        for load in loads:
+            load.wait()
 
     own_lane = lax.broadcasted_iota(jnp.int32, (HEADS, D), 1) // HD
     own_row = lax.broadcasted_iota(jnp.int32, (HEADS, D), 0)
     own_head = own_lane == own_row
     spot = (lax.broadcasted_iota(jnp.int32, (HEADS, CTX), 1) + CTX * t).astype(F32)
     stat_lane = lax.broadcasted_iota(jnp.int32, (HEADS, HD), 1)
-
-    done = 0
 
     def decode_slots_at(r):
         for plane in range(2):
@@ -490,20 +460,19 @@
             stat_row == a, query_sum, jnp.where(stat_row == 4 + a, key_sum, SS[q])
         )
 
-    turn_no = 0
-    for step in steps:
-        if step is None:
-            if turn_no == 2:
-                send_cache(1, 16)
-            turn_no += 1
-        else:
-            column_project(step)
-        if done < 8:
-            decode_slots_at(done)
-            done += 1
+    next(steps)
+    next(steps)
+    send_cache(8, 20)
+    column_project(next(steps))
+    decode_norms()
+    next(steps)
+    for r, column in enumerate(steps):
+        column_project(column)
+        if r < 2:
+            decode_slots_at(r)
     plane_peers(lambda chip, dev: remote(SS.at[q], SS.at[q], ms.at[6], mr.at[6], dev).start())
-    send_cache(16, 32)
-    for r in range(done, 8):
+    send_cache(20, 32)
+    for r in range(2, 8):
         decode_slots_at(r)
 
     OB[0] = OBF[0:16, :].astype(BF)
@@ -648,13 +617,24 @@
         DX2[q] = add_normed_row(DX[q], DR, 2)
         plane_peers(lambda chip, dev: remote(DX2.at[q], DX2.at[q], ms.at[9], mr.at[9], dev).start())
 
-    attn_rows = []
-    nothing = lambda: None
-    run(
-        reduce_steps(p, Y, RB1, r1s, r1r, sends, attn_rows, column_attend),
-        [nothing, nothing, hidden_row],
+    first_sum = Reduce(p, Y, RB1, r1s, r1r, sends)
+    for k in (3, 1, 2, 0):
+        column_attend(first_sum.columns[k])
+        first_sum.first_hop(k)
+        first_sum.leaves(k)
+        if k == 2:
+            first_sum.second_hop(3)
+    first_sum.second_hop(1)
+    first_sum.column_sum(3)
+    first_sum.second_hop(2)
+    first_sum.column_sum(1)
+    first_sum.second_hop(0)
+    first_sum.column_sum(2)
+    first_sum.column_sum(0)
+    hidden_row()
+    X2[own_block, :] = add_normed_rows(
+        X1[own_block, :].astype(F32), first_sum.own_sum(), 2
     )
-    X2[own_block, :] = add_normed_rows(X1[own_block, :].astype(F32), attn_rows[0], 2)
     steps = gather_steps(p, X2, g2s, g2r, sends)
     next(steps)
 
@@ -703,15 +683,6 @@
         new_prompt_kv[...] = NKV[...]
         new_decode_kv[0, 0:1, :] = own_row_of(KH[...])
         new_decode_kv[0, 1:2, :] = own_row_of(DKV[1].astype(F32))
-
-    tasks = [nothing, decode_ffn, fresh_out, final_row]
-    for step in steps:
-        if step is not None:
-            column_gated(step)
-        elif tasks:
-            tasks.pop(0)()
-    for task in tasks:
-        task()
 
     slot_of = lax.broadcasted_iota(jnp.int32, (32, 16, HD), 0) + 32 * y
     crossing = []
@@ -745,12 +716,31 @@
         for j in range(HEADS):
             decode_out[:, j * HD : (j + 1) * HD] = result[j : j + 1, :].astype(BF)
 
-    ffn_rows = []
-    run(
-        reduce_steps(p, Y2, RB2, r2s, r2r, sends, ffn_rows, column_down),
-        [cross_rows, nothing, nothing, decode_rows_out],
-    )
-    out_rows = add_normed_rows(X2[own_block, :].astype(F32), ffn_rows[0], 3)
+    second_sum = Reduce(p, Y2, RB2, r2s, r2r, sends)
+    tasks = [lambda: None, decode_ffn, fresh_out]
+    order = 0
+    for step in steps:
+        if step is not None:
+            column_gated(step)
+            column_down(step)
+            second_sum.first_hop(order)
+            second_sum.leaves(order)
+            order += 1
+            if order == 4:
+                second_sum.second_hop(0)
+        elif tasks:
+            tasks.pop(0)()
+    final_row()
+    second_sum.second_hop(1)
+    second_sum.second_hop(2)
+    second_sum.second_hop(3)
+    second_sum.column_sum(1)
+    second_sum.column_sum(2)
+    cross_rows()
+    second_sum.column_sum(3)
+    second_sum.column_sum(0)
+    decode_rows_out()
+    out_rows = add_normed_rows(X2[own_block, :].astype(F32), second_sum.own_sum(), 3)
     FS[...] = out_rows.reshape(2, 16, D)
     swap = remote(FS.at[1 - c], PO.at[c], ws.at[5], wr.at[5], sib)
     swap.start()
@@ -803,8 +793,8 @@
         ((512, D), BF),
         ((512, D), BF),
         ((512, D), BF),
-        ((30, 16, D), BF),
-        ((30, 16, D), BF),
+        ((480, D), BF),
+        ((480, D), BF),
         ((3, 2, 64, D), BF),
         ((2, 64, D), BF),
         ((2, 2, D, FFD), BF),

time: 117 us -> 114 us (0.974)
  Pallas kernels: 116 us -> 113 us
    pallas_call x1, Pallas kernels: 114 us -> 112 us  [local(): pl.pallas_call(kernel, out_shape=(jax.ShapeDtypeStruct((2, 16, D), BF), j...]
where the time goes in v3:
time: 114 us
  Pallas kernels  113 us (99%)
    pallas_call x1, Pallas kernels, local(): pl.pallas_call(kernel, out_shape=(jax.ShapeDtypeStruct((2, 16, D), BF), j...  112 us

profile of v3, /device:TPU:1, one launch (start us, length us, event | category | flops | bytes accessed | tf_op | source)
XLA Modules:
  0.0 114.1 jit_solution(13999496928091935562)
XLA Ops:
  0.6 111.7 %decoder_layer.1 = (bf16[2,16,2048]{2,1,0:T(8,128)(2,1)}, bf16[1,2048]{1,0:T(2,128)(2,1)}, bf16[2,2,16,2048]{3,2,1,0:T(8,128)(2,1)}, bf16[1,2,2048]{2,1,0:T(2,128)(2,1)}) custom-call(bf16[2,16,2048]{2,1,0:T(8,128)(2,1)} %prompt_states.1, bf16[1,2048]{1,0:T(2,128)(2,1)} %decode_states.1, bf16[2,34,48,2048]{3,2,1,0:T(8,128)(2,1)} %cache.1, s32[8]{0:T(128)} %prompt_starts.1, ...), custom_call_target="tpu_custom_call" | custom-call | tf_op jit(solution)/shard_map/decoder_layer/pallas_call | solution.py:837
  112.3 1.8 %place.1 = (bf16[2,16,2048]{2,1,0:T(8,128)(2,1)}, bf16[1,2048]{1,0:T(2,128)(2,1)}, bf16[2,2,16,2048]{3,2,1,0:T(8,128)(2,1)}, bf16[1,2,2048]{2,1,0:T(2,128)(2,1)}) custom-call(bf16[2,16,2048]{2,1,0:T(8,128)(2,1)} %get-tuple-element.12.refs_0_, bf16[1,2048]{1,0:T(2,128)(2,1)} %get-tuple-element.13.refs_1_, bf16[2,2,16,2048]{3,2,1,0:T(8,128)(2,1)} %get-tuple-element.14.refs_2_, ...), custom_call_target="tpu_custom_call" | custom-call | tf_op jit(solution)/shard_map/place/pallas_call | solution.py:868

commit v4 on v3

--- a/solution.py
+++ b/solution.py
@@ -357,7 +357,7 @@
             last,
         )
 
-    send_cache(1, 8)
+    send_cache(1, 14)
     piece_here.wait()
     piece.wait_recv()
     steps = gather_steps(p, X1, g1s, g1r, sends)
@@ -462,7 +462,7 @@
 
     next(steps)
     next(steps)
-    send_cache(8, 20)
+    send_cache(14, 32)
     column_project(next(steps))
     decode_norms()
     next(steps)
@@ -471,7 +471,6 @@
         if r < 2:
             decode_slots_at(r)
     plane_peers(lambda chip, dev: remote(SS.at[q], SS.at[q], ms.at[6], mr.at[6], dev).start())
-    send_cache(20, 32)
     for r in range(2, 8):
         decode_slots_at(r)
 

time: 114 us -> 118 us (1.035)
  Pallas kernels: 113 us -> 117 us
    pallas_call x1, Pallas kernels: 112 us -> 115 us  [local(): pl.pallas_call(kernel, out_shape=(jax.ShapeDtypeStruct((2, 16, D), BF), j...]
where the time goes in v4:
time: 118 us
  Pallas kernels  117 us (99%)
    pallas_call x1, Pallas kernels, local(): pl.pallas_call(kernel, out_shape=(jax.ShapeDtypeStruct((2, 16, D), BF), j...  115 us

profile of v4, /device:TPU:1, one launch (start us, length us, event | category | flops | bytes accessed | tf_op | source)
XLA Modules:
  0.0 117.7 jit_solution(5028669363461644693)
XLA Ops:
  0.6 115.3 %decoder_layer.1 = (bf16[2,16,2048]{2,1,0:T(8,128)(2,1)}, bf16[1,2048]{1,0:T(2,128)(2,1)}, bf16[2,2,16,2048]{3,2,1,0:T(8,128)(2,1)}, bf16[1,2,2048]{2,1,0:T(2,128)(2,1)}) custom-call(bf16[2,16,2048]{2,1,0:T(8,128)(2,1)} %prompt_states.1, bf16[1,2048]{1,0:T(2,128)(2,1)} %decode_states.1, bf16[2,34,48,2048]{3,2,1,0:T(8,128)(2,1)} %cache.1, s32[8]{0:T(128)} %prompt_starts.1, ...), custom_call_target="tpu_custom_call" | custom-call | tf_op jit(solution)/shard_map/decoder_layer/pallas_call | solution.py:836
  115.9 1.8 %place.1 = (bf16[2,16,2048]{2,1,0:T(8,128)(2,1)}, bf16[1,2048]{1,0:T(2,128)(2,1)}, bf16[2,2,16,2048]{3,2,1,0:T(8,128)(2,1)}, bf16[1,2,2048]{2,1,0:T(2,128)(2,1)}) custom-call(bf16[2,16,2048]{2,1,0:T(8,128)(2,1)} %get-tuple-element.12.refs_0_, bf16[1,2048]{1,0:T(2,128)(2,1)} %get-tuple-element.13.refs_1_, bf16[2,2,16,2048]{3,2,1,0:T(8,128)(2,1)} %get-tuple-element.14.refs_2_, ...), custom_call_target="tpu_custom_call" | custom-call | tf_op jit(solution)/shard_map/place/pallas_call | solution.py:867
